TPU v7x, 32 devices: a whole 2x2x4 slice. The times are simulated.
32 devices in a mesh: row: 16 (over z, y, core), col: 2 (over x).
Axes of the slice: x: 2, y: 2, z: 4, core: 2. Of those that a mesh axis runs over, the one named last changes fastest.
Arguments:
- features: bfloat16 [128, 4096], P(None, ('row', 'col')), may hold values from -6 to 6
- positions: float32 [3, 4096], P(None, ('row', 'col')), may hold values from 0 to 6
- tile_pairs: int32 [16, 2, 2, 4], P('row', 'col'), may hold values from 0 to 15, as said below
- pair_count: int32 [16, 2], P('row', 'col'), may hold values from 1 to 4, as said below
- masks: int32 [16, 2, 4, 128, 128], P('row', 'col'), may hold values 0 or 1
- w_in: bfloat16 [128, 128], replicated, may hold values from -0.5 to 0.5
- w_f1: bfloat16 [64, 128], replicated, may hold values from -3 to 3
- b_f1: float32 [128], replicated, may hold values from -3 to 3
- w_f2: bfloat16 [128, 128], replicated, may hold values from -0.1875 to 0.1875
- b_f2: float32 [128], replicated, may hold values from -2 to 2
- w_o1: bfloat16 [128, 128], replicated, may hold values from -0.25 to 0.25
- b_o1: float32 [128], replicated, may hold values from -3 to 3
- w_o2: bfloat16 [128, 128], replicated, may hold values from -0.5 to 0.5
- b_o2: float32 [128], replicated, may hold values from -3 to 3
- read_w: float32 [128], replicated, may hold values from -2 to 2
Outputs:
- features_out: bfloat16 [128, 4096], P(None, ('row', 'col'))
- forces: float32 [3, 4096], P(None, ('row', 'col'))
Inputs may be any that keep to these rules, and one draw needn't show every extreme that they name: Only slots 0 to pair_count[r, c] - 1 of tile_pairs and masks of block (r, c) are listed. tile_pairs[r, c, 0, s] is a receiver tile below 2, tile_pairs[r, c, 1, s] a sender tile below 16; the slots of one grid block hold distinct tile pairs.
All inputs are finite; a program needn't handle non-finite values. No bound on the sum of `masks` on one device may be relied on, other than what follows from the above.
Results may differ from a plain program's by a relative error of at most 0.0075.
Values may be sent and summed in bfloat16 or wider, within the bound.
No kernel may reach another device: no remote copies, remote signals or barrier semaphores. Data moves between devices by JAX's collectives and lax.ppermute only.
A program may use at most 64 MiB of HBM per device.

v0:
```python
import math

import jax
import jax.numpy as jnp
from jax import lax
from jax.sharding import PartitionSpec as P

SOFTENING = 0.25
GAMMA_RBF = 10.0
CENTER_MAX = 10.0
CUTOFF = 12.0


def shifted_softplus(value):
    return jax.nn.softplus(value) - math.log(2.0)


def filter_forward(distance, w_f1, b_f1, w_f2, b_f2):
    nbasis = w_f1.shape[0]
    centers = (jnp.arange(nbasis, dtype=jnp.float32) * (CENTER_MAX / (nbasis - 1)))[:, None, None]
    offset = distance[None] - centers
    gauss = jnp.exp(-GAMMA_RBF * offset * offset)
    basis = gauss.astype(jnp.bfloat16)
    hidden_pre = (
        jnp.einsum("kh,krc->hrc", w_f1, basis, preferred_element_type=jnp.float32)
        + b_f1[:, None, None]
    )
    hidden = shifted_softplus(hidden_pre).astype(jnp.bfloat16)
    filter_base = (
        jnp.einsum("hf,hrc->frc", w_f2, hidden, preferred_element_type=jnp.float32)
        + b_f2[:, None, None]
    )
    cutoff = 0.5 * (jnp.cos(math.pi / CUTOFF * distance) + 1.0)
    return (offset, gauss, hidden_pre, filter_base, cutoff)


def pair_geometry(pos_rows, pos_cols):
    separation = pos_rows[:, :, None] - pos_cols[:, None, :]
    distance = jnp.sqrt(jnp.sum(separation * separation, axis=0) + SOFTENING)
    return (separation, distance)


def tile_messages(pos_rows, pos_cols, sender_feats, pair_mask, params):
    separation, distance = pair_geometry(pos_rows, pos_cols)
    offset, gauss, hidden_pre, filter_base, cutoff = filter_forward(distance, *params)
    weighted = filter_base * (cutoff * pair_mask)[None]
    return jnp.sum(weighted * sender_feats.astype(jnp.float32)[:, None, :], axis=2)


def tile_forces(pos_rows, pos_cols, sender_feats, grad_rows, pair_mask, params):
    w_f1, b_f1, w_f2, b_f2 = params
    separation, distance = pair_geometry(pos_rows, pos_cols)
    offset, gauss, hidden_pre, filter_base, cutoff = filter_forward(distance, *params)
    pair_grad = (
        grad_rows[:, :, None] * sender_feats.astype(jnp.float32)[:, None, :] * pair_mask[None]
    )
    filter_grad = (pair_grad * cutoff[None]).astype(jnp.bfloat16)
    cutoff_grad = jnp.sum(pair_grad * filter_base, axis=0)
    hidden_grad = jnp.einsum("hf,frc->hrc", w_f2, filter_grad, preferred_element_type=jnp.float32)
    hidden_grad = (hidden_grad * jax.nn.sigmoid(hidden_pre)).astype(jnp.bfloat16)
    basis_grad = jnp.einsum("kh,hrc->krc", w_f1, hidden_grad, preferred_element_type=jnp.float32)
    dist_grad = -2.0 * GAMMA_RBF * jnp.sum(basis_grad * gauss * offset, axis=0)
    dist_grad = (
        dist_grad - 0.5 * math.pi / CUTOFF * jnp.sin(math.pi / CUTOFF * distance) * cutoff_grad
    )
    push = separation * (dist_grad / distance)[None]
    return (-jnp.sum(push, axis=2), jnp.sum(push, axis=1))


def atom_update(messages, w_o1, b_o1, w_o2, b_o2, read_w):
    pre_act = (
        jnp.einsum(
            "fo,fa->oa", w_o1, messages.astype(jnp.bfloat16), preferred_element_type=jnp.float32
        )
        + b_o1[:, None]
    )
    activated = shifted_softplus(pre_act).astype(jnp.bfloat16)
    update = (
        jnp.einsum("fo,fa->oa", w_o2, activated, preferred_element_type=jnp.float32) + b_o2[:, None]
    )
    direction = jnp.dot(w_o2.astype(jnp.float32), read_w, precision=lax.Precision.HIGHEST)
    message_grad = jnp.dot(
        w_o1.astype(jnp.float32),
        direction[:, None] * jax.nn.sigmoid(pre_act),
        precision=lax.Precision.HIGHEST,
    )
    return (update, message_grad)


def local(
    features,
    positions,
    tile_pairs,
    pair_count,
    masks,
    w_in,
    w_f1,
    b_f1,
    w_f2,
    b_f2,
    w_o1,
    b_o1,
    w_o2,
    b_o2,
    read_w,
):
    params = (w_f1, b_f1, w_f2, b_f2)
    owned = features.shape[1]
    tile = masks.shape[-1]
    row_count = lax.axis_size("row")
    col_count = lax.axis_size("col")
    row_index = lax.axis_index("row")
    col_index = lax.axis_index("col")
    row_span = col_count * owned
    projected = jnp.einsum("fo,fa->oa", w_in, features, preferred_element_type=jnp.float32).astype(
        jnp.bfloat16
    )
    sender_block = lax.all_gather(projected, "row", axis=1, tiled=True)
    every_position = lax.all_gather(positions, ("row", "col"), axis=1, tiled=True)
    row_positions = lax.dynamic_slice_in_dim(every_position, row_index * row_span, row_span, 1)
    col_positions = lax.dynamic_index_in_dim(
        every_position.reshape(3, row_count, col_count, owned), col_index, 2, keepdims=False
    )
    col_positions = col_positions.reshape(3, row_count * owned)
    slot_pairs = tile_pairs[0, 0]
    slot_masks = masks[0, 0]
    pair_total = pair_count[0, 0]

    def locate(slot_index):
        row_start = slot_pairs[0, slot_index] * tile
        col_start = slot_pairs[1, slot_index] * tile
        pair_mask = lax.dynamic_index_in_dim(slot_masks, slot_index, 0, keepdims=False).astype(
            jnp.float32
        )
        return (row_start, col_start, pair_mask)

    def forward_slot(slot_index, totals):
        row_start, col_start, pair_mask = locate(slot_index)
        tile_sum = tile_messages(
            lax.dynamic_slice_in_dim(row_positions, row_start, tile, 1),
            lax.dynamic_slice_in_dim(col_positions, col_start, tile, 1),
            lax.dynamic_slice_in_dim(sender_block, col_start, tile, 1),
            pair_mask,
            params,
        )
        current = lax.dynamic_slice_in_dim(totals, row_start, tile, 1)
        return lax.dynamic_update_slice_in_dim(totals, current + tile_sum, row_start, 1)

    partial_messages = lax.fori_loop(
        jnp.int32(0),
        pair_total,
        forward_slot,
        jnp.zeros((projected.shape[0], row_span), jnp.float32),
    )
    block_messages_sum = lax.psum(partial_messages, "col")
    block_update, message_grad = atom_update(block_messages_sum, w_o1, b_o1, w_o2, b_o2, read_w)
    update = lax.dynamic_slice_in_dim(block_update, col_index * owned, owned, 1)
    features_out = (features.astype(jnp.float32) + update).astype(jnp.bfloat16)

    def backward_slot(slot_index, carried):
        row_force, col_force = carried
        row_start, col_start, pair_mask = locate(slot_index)
        row_part, col_part = tile_forces(
            lax.dynamic_slice_in_dim(row_positions, row_start, tile, 1),
            lax.dynamic_slice_in_dim(col_positions, col_start, tile, 1),
            lax.dynamic_slice_in_dim(sender_block, col_start, tile, 1),
            lax.dynamic_slice_in_dim(message_grad, row_start, tile, 1),
            pair_mask,
            params,
        )
        current = lax.dynamic_slice_in_dim(row_force, row_start, tile, 1)
        row_force = lax.dynamic_update_slice_in_dim(row_force, current + row_part, row_start, 1)
        current = lax.dynamic_slice_in_dim(col_force, col_start, tile, 1)
        col_force = lax.dynamic_update_slice_in_dim(col_force, current + col_part, col_start, 1)
        return (row_force, col_force)

    row_force, col_force = lax.fori_loop(
        jnp.int32(0),
        pair_total,
        backward_slot,
        (jnp.zeros((3, row_span), jnp.float32), jnp.zeros((3, row_count * owned), jnp.float32)),
    )
    receiver_side = lax.psum_scatter(row_force, "col", scatter_dimension=1, tiled=True)
    sender_side = lax.psum_scatter(col_force, "row", scatter_dimension=1, tiled=True)
    return (features_out, receiver_side + sender_side)


def solution(mesh):
    in_specs = (
        P(None, ("row", "col")),
        P(None, ("row", "col")),
        P("row", "col", None, None),
        P("row", "col"),
        P("row", "col", None, None, None),
        P(),
        P(),
        P(),
        P(),
        P(),
        P(),
        P(),
        P(),
        P(),
        P(),
    )
    out_specs = (P(None, ("row", "col")), P(None, ("row", "col")))
    return jax.shard_map(local, mesh=mesh, in_specs=in_specs, out_specs=out_specs, check_vma=False)
```

profile of v0, /device:TPU:0, one launch (start us, length us, event | category | flops | bytes accessed | tf_op | source)
XLA Modules:
  0.0 355.7 jit_solution(15952742850979216977)
XLA Ops:
  7.2 0.9 copy.48
  8.1 70.2 %all_gather.6 = f32[3,4096]{1,0:T(4,128)S(1)} all-gather(f32[3,128]{1,0:T(4,128)} %param.20), channel_id=1, replica_groups=mesh['row'=16,'col'=2] {'row','col'}, dimensions={1}, use_global_device_ids=true | all-gather | bytes 50688 | tf_op jit(solution)/shard_map/all_gather | solution.py:119
  78.5 1.0 convolution_convert_fusion
  79.4 18.7 %all_gather.7 = bf16[128,2048]{1,0:T(8,128)(2,1)S(1)} all-gather(bf16[128,128]{1,0:T(8,128)(2,1)S(1)} %convolution_convert_fusion), channel_id=1, replica_groups=mesh['row'=16,'col'=2] {'row'}, dimensions={1}, use_global_device_ids=true | all-gather | bytes 557056 | tf_op jit(solution)/shard_map/all_gather | solution.py:118
  98.2 53.9 %while.26 = (s32[]{:T(128)}, f32[128,256]{0,1:T(8,128)S(1)}, s32[]{:T(128)}, s32[2,4]{1,0:T(2,128)}, f32[3,256]{1,0:T(4,128)S(1)}, /*index=5*/f32[3,2048]{1,0:T(...) while((s32[]{:T(128)}, f32[128,256]{0,1:T(8,128)S(1)}, ...), condition=%wide.region_3.4_spmd, body=%wide.region_0.3_spmd.sunk | while | flops 837025856 | bytes 1141587 | solution.py:149
  98.9 1.4 constant_dynamic-slice_fusion.21
  101.9 1.1 fusion.132
  103.0 8.5 %fusion.133 = f32[128,128]{0,1:T(8,128)S(1)} fusion(f32[128,128]{0,1:T(8,128)S(1)} %convert_element_type.134, f32[128,128]{1,0:T(8,128)S(1)} %fusion.132, f32[128]{0:T(128)} %get-tuple-element.739, f32[128]{0:T(128)} %get-tuple-element.737, f32[64]{0:T(128)S(1)} %iota_multiply_fusion.4, f32[128,128]{1,0:T(8,128)S(1)} %add_sqrt_fusion.3, ...), kind=kOutput, calls=%fused_computation.4.clone.1 | convolution fusion | flops 836747264 | bytes 312576 | tf_op jit(solution)/shard_map/while/body/hf,hrc->frc/dot_general | solution.py:30
  112.2 1.4 constant_dynamic-slice_fusion.21
  115.2 1.1 fusion.132
  116.3 8.5 %fusion.133 = f32[128,128]{0,1:T(8,128)S(1)} fusion(f32[128,128]{0,1:T(8,128)S(1)} %convert_element_type.134, f32[128,128]{1,0:T(8,128)S(1)} %fusion.132, f32[128]{0:T(128)} %get-tuple-element.739, f32[128]{0:T(128)} %get-tuple-element.737, f32[64]{0:T(128)S(1)} %iota_multiply_fusion.4, f32[128,128]{1,0:T(8,128)S(1)} %add_sqrt_fusion.3, ...), kind=kOutput, calls=%fused_computation.4.clone.1 | convolution fusion | flops 836747264 | bytes 312576 | tf_op jit(solution)/shard_map/while/body/hf,hrc->frc/dot_general | solution.py:30
  125.5 1.4 constant_dynamic-slice_fusion.21
  128.5 1.1 fusion.132
  129.6 8.5 %fusion.133 = f32[128,128]{0,1:T(8,128)S(1)} fusion(f32[128,128]{0,1:T(8,128)S(1)} %convert_element_type.134, f32[128,128]{1,0:T(8,128)S(1)} %fusion.132, f32[128]{0:T(128)} %get-tuple-element.739, f32[128]{0:T(128)} %get-tuple-element.737, f32[64]{0:T(128)S(1)} %iota_multiply_fusion.4, f32[128,128]{1,0:T(8,128)S(1)} %add_sqrt_fusion.3, ...), kind=kOutput, calls=%fused_computation.4.clone.1 | convolution fusion | flops 836747264 | bytes 312576 | tf_op jit(solution)/shard_map/while/body/hf,hrc->frc/dot_general | solution.py:30
  138.8 1.4 constant_dynamic-slice_fusion.21
  141.8 1.1 fusion.132
  142.9 8.5 %fusion.133 = f32[128,128]{0,1:T(8,128)S(1)} fusion(f32[128,128]{0,1:T(8,128)S(1)} %convert_element_type.134, f32[128,128]{1,0:T(8,128)S(1)} %fusion.132, f32[128]{0:T(128)} %get-tuple-element.739, f32[128]{0:T(128)} %get-tuple-element.737, f32[64]{0:T(128)S(1)} %iota_multiply_fusion.4, f32[128,128]{1,0:T(8,128)S(1)} %add_sqrt_fusion.3, ...), kind=kOutput, calls=%fused_computation.4.clone.1 | convolution fusion | flops 836747264 | bytes 312576 | tf_op jit(solution)/shard_map/while/body/hf,hrc->frc/dot_general | solution.py:30
  152.1 8.2 %all-reduce.1 = bf16[128,256]{0,1:T(8,128)(2,1)S(1)} all-reduce(f32[128,256]{0,1:T(8,128)S(1)} %get-tuple-element.331), channel_id=1, replica_groups=mesh['row'=16,'col'=2] {'col'}, use_global_device_ids=true, to_apply=%region_4.5 | all-reduce | flops 32768 | bytes 196608 | tf_op jit(solution)/shard_map/psum | solution.py:155
  160.9 118.2 %while.27 = (s32[]{:T(128)}, f32[3,256]{1,0:T(4,128)S(1)}, f32[3,2048]{1,0:T(4,128)S(1)}, s32[]{:T(128)}, s32[2,4]{1,0:T(2,128)}, /*index=5*/f32[3,256]{1,0:T(4,...) while((s32[]{:T(128)}, f32[3,256]{1,0:T(4,128)S(1)}, ...), condition=%wide.region_11.12_spmd, body=%wide.region_5.11_spmd.sunk | while | flops 1671938432 | bytes 27035328 | solution.py:177
  161.8 1.4 constant_dynamic-slice_fusion.24
  164.6 0.9 convert_bitcast_fusion.2
  165.9 5.3 %fusion.142 = f32[128,128,128]{2,1,0:T(8,128)} fusion(f32[64]{0:T(128)S(1)} %iota_multiply_fusion.5, f32[128,128]{1,0:T(8,128)S(1)} %get-tuple-element.688, bf16[64,128]{1,0:T(8,128)(2,1)} %get-tuple-element.799), kind=kOutput, calls=%fused_computation.68.clone.1 | convolution fusion | flops 272629760 | bytes 8470784 | tf_op jit(solution)/shard_map/while/body/kh,krc->hrc/dot_general | solution.py:25
  171.3 9.3 %fusion.144 = f32[128,128]{1,0:T(8,128)S(1)} fusion(f32[64]{0:T(128)S(1)} %iota_multiply_fusion.5, f32[128,128]{1,0:T(8,128)S(1)} %get-tuple-element.688, f32[128,128,128]{2,1,0:T(8,128)} %fusion.142, f32[128]{0:T(128)S(1)} %copy-done.7, f32[128,128]{1,0:T(8,128)S(1)} %get-tuple-element.689, f32[128,128]{1,0:T(8,128)S(1)} %convert_bitcast_fusion.2, ...), kind=kOutput, calls=%fused_computation.60.clone.1 | convolution fusion | flops 832552960 | bytes 8831744 | tf_op jit(solution)/shard_map/while/body/kh,hrc->krc/dot_general | solution.py:61
  180.6 9.3 %fusion.143 = f32[128,128]{1,0:T(8,128)S(1)} fusion(f32[128]{0:T(128)S(1)} %copy-done.8, f32[128,128]{1,0:T(8,128)S(1)} %convert_bitcast_fusion.2, f32[128,128]{1,0:T(8,128)S(1)} %dynamic-slice_convert_fusion.2, f32[128,128]{0,1:T(8,128)S(1)} %constant_dynamic-slice_fusion.25, f32[128,128,128]{2,1,0:T(8,128)} %fusion.142, f32[128]{0:T(128)S(1)} %copy-done.7, ...), kind=kOutput, calls=%fused_computation.39.clone.1 | convolution fusion | flops 566214656 | bytes 8684544 | tf_op jit(solution)/shard_map/while/body/hf,hrc->frc/dot_general | solution.py:30
  189.9 0.3 subtract_divide_fusion.2
  191.2 1.4 constant_dynamic-slice_fusion.24
  194.0 0.9 convert_bitcast_fusion.2
  195.3 5.3 %fusion.142 = f32[128,128,128]{2,1,0:T(8,128)} fusion(f32[64]{0:T(128)S(1)} %iota_multiply_fusion.5, f32[128,128]{1,0:T(8,128)S(1)} %get-tuple-element.688, bf16[64,128]{1,0:T(8,128)(2,1)} %get-tuple-element.799), kind=kOutput, calls=%fused_computation.68.clone.1 | convolution fusion | flops 272629760 | bytes 8470784 | tf_op jit(solution)/shard_map/while/body/kh,krc->hrc/dot_general | solution.py:25
  200.6 9.3 %fusion.144 = f32[128,128]{1,0:T(8,128)S(1)} fusion(f32[64]{0:T(128)S(1)} %iota_multiply_fusion.5, f32[128,128]{1,0:T(8,128)S(1)} %get-tuple-element.688, f32[128,128,128]{2,1,0:T(8,128)} %fusion.142, f32[128]{0:T(128)S(1)} %copy-done.7, f32[128,128]{1,0:T(8,128)S(1)} %get-tuple-element.689, f32[128,128]{1,0:T(8,128)S(1)} %convert_bitcast_fusion.2, ...), kind=kOutput, calls=%fused_computation.60.clone.1 | convolution fusion | flops 832552960 | bytes 8831744 | tf_op jit(solution)/shard_map/while/body/kh,hrc->krc/dot_general | solution.py:61
  209.9 9.3 %fusion.143 = f32[128,128]{1,0:T(8,128)S(1)} fusion(f32[128]{0:T(128)S(1)} %copy-done.8, f32[128,128]{1,0:T(8,128)S(1)} %convert_bitcast_fusion.2, f32[128,128]{1,0:T(8,128)S(1)} %dynamic-slice_convert_fusion.2, f32[128,128]{0,1:T(8,128)S(1)} %constant_dynamic-slice_fusion.25, f32[128,128,128]{2,1,0:T(8,128)} %fusion.142, f32[128]{0:T(128)S(1)} %copy-done.7, ...), kind=kOutput, calls=%fused_computation.39.clone.1 | convolution fusion | flops 566214656 | bytes 8684544 | tf_op jit(solution)/shard_map/while/body/hf,hrc->frc/dot_general | solution.py:30
  220.5 1.4 constant_dynamic-slice_fusion.24
  223.3 0.9 convert_bitcast_fusion.2
  224.6 5.3 %fusion.142 = f32[128,128,128]{2,1,0:T(8,128)} fusion(f32[64]{0:T(128)S(1)} %iota_multiply_fusion.5, f32[128,128]{1,0:T(8,128)S(1)} %get-tuple-element.688, bf16[64,128]{1,0:T(8,128)(2,1)} %get-tuple-element.799), kind=kOutput, calls=%fused_computation.68.clone.1 | convolution fusion | flops 272629760 | bytes 8470784 | tf_op jit(solution)/shard_map/while/body/kh,krc->hrc/dot_general | solution.py:25
  230.0 9.3 %fusion.144 = f32[128,128]{1,0:T(8,128)S(1)} fusion(f32[64]{0:T(128)S(1)} %iota_multiply_fusion.5, f32[128,128]{1,0:T(8,128)S(1)} %get-tuple-element.688, f32[128,128,128]{2,1,0:T(8,128)} %fusion.142, f32[128]{0:T(128)S(1)} %copy-done.7, f32[128,128]{1,0:T(8,128)S(1)} %get-tuple-element.689, f32[128,128]{1,0:T(8,128)S(1)} %convert_bitcast_fusion.2, ...), kind=kOutput, calls=%fused_computation.60.clone.1 | convolution fusion | flops 832552960 | bytes 8831744 | tf_op jit(solution)/shard_map/while/body/kh,hrc->krc/dot_general | solution.py:61
  239.3 9.3 %fusion.143 = f32[128,128]{1,0:T(8,128)S(1)} fusion(f32[128]{0:T(128)S(1)} %copy-done.8, f32[128,128]{1,0:T(8,128)S(1)} %convert_bitcast_fusion.2, f32[128,128]{1,0:T(8,128)S(1)} %dynamic-slice_convert_fusion.2, f32[128,128]{0,1:T(8,128)S(1)} %constant_dynamic-slice_fusion.25, f32[128,128,128]{2,1,0:T(8,128)} %fusion.142, f32[128]{0:T(128)S(1)} %copy-done.7, ...), kind=kOutput, calls=%fused_computation.39.clone.1 | convolution fusion | flops 566214656 | bytes 8684544 | tf_op jit(solution)/shard_map/while/body/hf,hrc->frc/dot_general | solution.py:30
  249.8 1.4 constant_dynamic-slice_fusion.24
  252.7 0.9 convert_bitcast_fusion.2
  253.9 5.3 %fusion.142 = f32[128,128,128]{2,1,0:T(8,128)} fusion(f32[64]{0:T(128)S(1)} %iota_multiply_fusion.5, f32[128,128]{1,0:T(8,128)S(1)} %get-tuple-element.688, bf16[64,128]{1,0:T(8,128)(2,1)} %get-tuple-element.799), kind=kOutput, calls=%fused_computation.68.clone.1 | convolution fusion | flops 272629760 | bytes 8470784 | tf_op jit(solution)/shard_map/while/body/kh,krc->hrc/dot_general | solution.py:25
  259.3 9.3 %fusion.144 = f32[128,128]{1,0:T(8,128)S(1)} fusion(f32[64]{0:T(128)S(1)} %iota_multiply_fusion.5, f32[128,128]{1,0:T(8,128)S(1)} %get-tuple-element.688, f32[128,128,128]{2,1,0:T(8,128)} %fusion.142, f32[128]{0:T(128)S(1)} %copy-done.7, f32[128,128]{1,0:T(8,128)S(1)} %get-tuple-element.689, f32[128,128]{1,0:T(8,128)S(1)} %convert_bitcast_fusion.2, ...), kind=kOutput, calls=%fused_computation.60.clone.1 | convolution fusion | flops 832552960 | bytes 8831744 | tf_op jit(solution)/shard_map/while/body/kh,hrc->krc/dot_general | solution.py:61
  268.6 9.3 %fusion.143 = f32[128,128]{1,0:T(8,128)S(1)} fusion(f32[128]{0:T(128)S(1)} %copy-done.8, f32[128,128]{1,0:T(8,128)S(1)} %convert_bitcast_fusion.2, f32[128,128]{1,0:T(8,128)S(1)} %dynamic-slice_convert_fusion.2, f32[128,128]{0,1:T(8,128)S(1)} %constant_dynamic-slice_fusion.25, f32[128,128,128]{2,1,0:T(8,128)} %fusion.142, f32[128]{0:T(128)S(1)} %copy-done.7, ...), kind=kOutput, calls=%fused_computation.39.clone.1 | convolution fusion | flops 566214656 | bytes 8684544 | tf_op jit(solution)/shard_map/while/body/hf,hrc->frc/dot_general | solution.py:30
  279.1 0.8 copy.55
  280.0 1.4 copy.57
  281.8 0.7 copy.49
  282.5 3.8 %reduce-scatter.7.cloned.1.call-done = f32[128,3]{1,0:T(8,128)} async-done(((f32[256,3]{1,0:T(8,128)}), f32[128,3]{1,0:T(8,128)}) %reduce-scatter.7.cloned.1.call-update) | async-done | bytes 1552
  286.3 0.9 copy.56
  287.2 60.2 %reduce-scatter.9.cloned.1.call-done = f32[128,3]{1,0:T(8,128)} async-done(((f32[2048,3]{1,0:T(8,128)}), f32[128,3]{1,0:T(8,128)}) %reduce-scatter.9.cloned.1.call-update) | async-done | bytes 1552
  347.3 0.9 copy.58
  348.2 0.6 add.299
  (124 shorter events, 6.0 us)
Async XLA Ops:
  7.2 153.3 %copy-start = (bf16[128,128]{1,0:T(8,128)(2,1)S(1)}, bf16[128,128]{1,0:T(8,128)(2,1)}, u32[]{:S(2)}) copy-start(bf16[128,128]{1,0:T(8,128)(2,1)} %param.29) | copy-start | bytes 98308
  7.2 279.1 %reduce-scatter.7.cloned.1.call-start = ((), (), s32[]{:S(2)}) async-start(), calls=%async_computation.2 | async-start | bytes 196608
  98.2 62.1 %copy-start.3 = (bf16[128,128]{1,0:T(8,128)(2,1)S(1)}, bf16[128,128]{1,0:T(8,128)(2,1)}, u32[]{:S(2)}) copy-start(bf16[128,128]{1,0:T(8,128)(2,1)} %param.31) | copy-start | bytes 98308
  98.2 62.1 %copy-start.4 = (f32[128]{0:T(128)S(1)}, f32[128]{0:T(128)}, u32[]{:S(2)}) copy-start(f32[128]{0:T(128)} %param.33) | copy-start | bytes 1540
  98.2 62.3 %copy-start.5 = (f32[128]{0:T(128)S(1)}, f32[128]{0:T(128)}, u32[]{:S(2)}) copy-start(f32[128]{0:T(128)} %param.30) | copy-start | bytes 1540
  160.9 120.5 %copy-start.2 = (bf16[128,128]{1,0:T(8,128)(2,1)S(1)}, bf16[128,128]{1,0:T(8,128)(2,1)}, u32[]{:S(2)}) copy-start(bf16[128,128]{1,0:T(8,128)(2,1)} %param.19) | copy-start | bytes 98308
  160.9 120.8 %copy-start.6 = (f32[128]{0:T(128)S(1)}, f32[128]{0:T(128)}, u32[]{:S(2)}) copy-start(f32[128]{0:T(128)} %param.32) | copy-start | bytes 1540
  161.8 9.5 %copy-start.1 = (bf16[64,128]{1,0:T(8,128)(2,1)S(1)}, bf16[64,128]{1,0:T(8,128)(2,1)}, u32[]{:S(2)}) copy-start(bf16[64,128]{1,0:T(8,128)(2,1)} %get-tuple-element.799) | copy-start | bytes 49156 | tf_op jit(solution)/shard_map/while
  161.8 9.5 %copy-start.7 = (f32[128]{0:T(128)S(1)}, f32[128]{0:T(128)}, u32[]{:S(2)}) copy-start(f32[128]{0:T(128)} %get-tuple-element.800) | copy-start | bytes 1540 | tf_op jit(solution)/shard_map/while
  171.3 9.3 %copy-start.8 = (f32[128]{0:T(128)S(1)}, f32[128]{0:T(128)}, u32[]{:S(2)}) copy-start(f32[128]{0:T(128)} %get-tuple-element.801) | copy-start | bytes 1540 | tf_op jit(solution)/shard_map/while
  191.1 9.5 %copy-start.1 = (bf16[64,128]{1,0:T(8,128)(2,1)S(1)}, bf16[64,128]{1,0:T(8,128)(2,1)}, u32[]{:S(2)}) copy-start(bf16[64,128]{1,0:T(8,128)(2,1)} %get-tuple-element.799) | copy-start | bytes 49156 | tf_op jit(solution)/shard_map/while
  191.1 9.5 %copy-start.7 = (f32[128]{0:T(128)S(1)}, f32[128]{0:T(128)}, u32[]{:S(2)}) copy-start(f32[128]{0:T(128)} %get-tuple-element.800) | copy-start | bytes 1540 | tf_op jit(solution)/shard_map/while
  200.6 9.3 %copy-start.8 = (f32[128]{0:T(128)S(1)}, f32[128]{0:T(128)}, u32[]{:S(2)}) copy-start(f32[128]{0:T(128)} %get-tuple-element.801) | copy-start | bytes 1540 | tf_op jit(solution)/shard_map/while
  220.5 9.5 %copy-start.1 = (bf16[64,128]{1,0:T(8,128)(2,1)S(1)}, bf16[64,128]{1,0:T(8,128)(2,1)}, u32[]{:S(2)}) copy-start(bf16[64,128]{1,0:T(8,128)(2,1)} %get-tuple-element.799) | copy-start | bytes 49156 | tf_op jit(solution)/shard_map/while
  220.5 9.5 %copy-start.7 = (f32[128]{0:T(128)S(1)}, f32[128]{0:T(128)}, u32[]{:S(2)}) copy-start(f32[128]{0:T(128)} %get-tuple-element.800) | copy-start | bytes 1540 | tf_op jit(solution)/shard_map/while
  230.0 9.3 %copy-start.8 = (f32[128]{0:T(128)S(1)}, f32[128]{0:T(128)}, u32[]{:S(2)}) copy-start(f32[128]{0:T(128)} %get-tuple-element.801) | copy-start | bytes 1540 | tf_op jit(solution)/shard_map/while
  249.8 9.5 %copy-start.1 = (bf16[64,128]{1,0:T(8,128)(2,1)S(1)}, bf16[64,128]{1,0:T(8,128)(2,1)}, u32[]{:S(2)}) copy-start(bf16[64,128]{1,0:T(8,128)(2,1)} %get-tuple-element.799) | copy-start | bytes 49156 | tf_op jit(solution)/shard_map/while
  249.8 9.5 %copy-start.7 = (f32[128]{0:T(128)S(1)}, f32[128]{0:T(128)}, u32[]{:S(2)}) copy-start(f32[128]{0:T(128)} %get-tuple-element.800) | copy-start | bytes 1540 | tf_op jit(solution)/shard_map/while
  259.3 9.3 %copy-start.8 = (f32[128]{0:T(128)S(1)}, f32[128]{0:T(128)}, u32[]{:S(2)}) copy-start(f32[128]{0:T(128)} %get-tuple-element.801) | copy-start | bytes 1540 | tf_op jit(solution)/shard_map/while
  280.0 67.4 %reduce-scatter.9.cloned.1.call-start = ((), (), s32[]{:S(2)}) async-start(), calls=%async_computation.3 | async-start | bytes 1114112
Sparse Core Ops, SparseCore 0:
  280.1 6.1 reduce-scatter.6
  289.9 57.4 reduce-scatter.8
where the time goes:
time: 356 us
  matrix products  132 us (37%)
  blocking collectives  97.2 us (27%)
  waiting for transfers between devices  64 us (18%)
  local copies, waits for them, and re-layouts  18 us (5%)
  loops' own time  17.9 us (5%)
  between operations  14.2 us (4%)
  other arithmetic  12.7 us (4%)
    dot_general x8, matrix products, filter_forward(): jnp.einsum('hf,hrc->frc', w_f2, hidden, preferred_element_type=jnp.float32)  71.3 us
    all_gather x1, blocking collectives, local(): lax.all_gather(positions, ('row', 'col'), axis=1, tiled=True)  70.2 us
    unnamed x4, waiting for transfers between devices  64 us
    dot_general x4, matrix products, tile_forces(): jnp.einsum('kh,hrc->krc', w_f1, hidden_grad, preferred_element_type=jnp.f...  37.2 us
    dot_general x4, matrix products, filter_forward(): jnp.einsum('kh,krc->hrc', w_f1, basis, preferred_element_type=jnp.float32)  21.4 us
    all_gather x1, blocking collectives, local(): sender_block = lax.all_gather(projected, 'row', axis=1, tiled=True)  18.7 us
    dynamic_slice x8, local copies, waits for them, and re-layouts, locate(): col_start = slot_pairs[1, slot_index] * tile  11.4 us
    another operation x1, loops' own time, local(): lax.fori_loop(jnp.int32(0), pair_total, backward_slot, (jnp.zeros((3, row...  9.31 us
  transfers between devices with their start and end apart: 2, of which 2 were waited for; matrix products, arithmetic and copies ran while one was open for 1% of the time, Pallas kernels for 0%

commit v1 on v0

v1 whole, which is shorter than its diff:
```python
import functools
import math

import jax
import jax.numpy as jnp
from jax import lax
from jax.experimental import pallas as pl
from jax.experimental.pallas import tpu as pltpu
from jax.sharding import PartitionSpec as P

SOFTENING = 0.25
GAMMA_RBF = 10.0
CENTER_MAX = 10.0
CUTOFF = 12.0
LOG2E = math.log2(math.e)
SCALE = math.sqrt(GAMMA_RBF * LOG2E)
TANGENT = -GAMMA_RBF / (SCALE * LOG2E)
POS_ROWS = 16
CHUNK = 16
F32 = jnp.float32
BF16 = jnp.bfloat16


def dot(a, b):
    return jnp.dot(a, b, preferred_element_type=F32)


def dot_t(a, b):
    return lax.dot_general(a, b, (((1,), (1,)), ((), ())), preferred_element_type=F32)


def split2(x):
    hi = x.astype(BF16)
    return hi, (x - hi.astype(F32)).astype(BF16)


def fold(x):
    half = x.shape[0] // 2
    return jnp.concatenate([x[:half], x[half:]], axis=1)


def unfold(x):
    half = x.shape[1] // 2
    return jnp.concatenate([x[:, :half], x[:, half:]], axis=0)


def block_diag(x):
    zero = jnp.zeros_like(x)
    return jnp.concatenate(
        [jnp.concatenate([x, zero], axis=1), jnp.concatenate([zero, x], axis=1)], axis=0
    )


def reverse_bits(value, count):
    bits = count.bit_length() - 1
    out = jnp.int32(0)
    for k in range(bits):
        out = out | (((value >> k) & 1) << (bits - 1 - k))
    return out


def pair_kernel(
    n_row, info, near, far, col_pos, masks, w_in, w_f1, b_f1, w_f2, b_f2,
    msg, tangents, proj_out, geom_out,
    lhs, w2, w_in_t, diag, dist, coef_h, coef_x, coef_t, rows,
):
    slot, chunk = pl.program_id(0), pl.program_id(1)
    nbasis = w_f1.shape[0]
    hidden = w_f1.shape[1]
    tile = masks.shape[-1]
    tp = masks.shape[0]

    @pl.when((slot == 0) & (chunk == 0))
    def _():
        weights = w_f1[...].astype(F32)
        zero = jnp.zeros_like(weights)
        bias = b_f1[...] * LOG2E - 1.0
        b_hi = bias.astype(BF16).astype(F32)
        b_mid = (bias - b_hi).astype(BF16).astype(F32)
        b_lo = bias - b_hi - b_mid
        extra = jnp.concatenate([b_hi, b_mid, b_lo, jnp.zeros((13, hidden), F32)], axis=0)
        table = jnp.concatenate(
            [
                jnp.concatenate([weights, zero], axis=1),
                jnp.concatenate([zero, weights], axis=1),
                jnp.concatenate([extra, jnp.zeros_like(extra)], axis=1),
                jnp.zeros((256 - 2 * nbasis - 16, 2 * hidden), F32),
            ],
            axis=0,
        )
        lhs[...] = table.T[:, : 2 * nbasis + 16].astype(BF16)
        wide = w_f2[...].astype(F32)
        w2[...] = jnp.concatenate([wide, wide], axis=1)
        w_in_t[...] = w_in[...].astype(F32).T.astype(BF16)
        msg[...] = jnp.zeros_like(msg)

    @pl.when(slot < info[2])
    def _():
        @pl.when(chunk == 0)
        def _():
            row_tile, col_tile = info[3 + slot], info[3 + tp + slot]
            place = reverse_bits(col_tile ^ info[0], n_row)
            half = n_row // 2
            index = place & (half - 1)
            block = jnp.where(place >= half, far[index], near[index])
            proj = dot(w_in_t[...], block[:tile]).astype(BF16)
            proj_out[0] = proj
            proj_t = proj.astype(F32).T.astype(BF16)
            diag[...] = block_diag(proj_t)
            pieces = block[tile:].astype(F32)
            sender = pieces[0:3] + pieces[3:6] + pieces[6:9]
            receiver = col_pos[row_tile ^ info[1]]
            square = jnp.zeros((tile, tile), F32)
            separation = []
            for k in range(3):
                up = jnp.broadcast_to(receiver[k : k + 1], (tile, tile)).T
                separation.append(up - sender[k : k + 1])
                square = square + separation[k] * separation[k]
            distance = jnp.sqrt(square + SOFTENING)
            angle = (math.pi / CUTOFF) * distance
            mask = masks[slot].astype(F32)
            cut = 0.5 * (jnp.cos(angle) + 1.0) * mask
            slope = (-0.5 * math.pi / CUTOFF) * jnp.sin(angle) * mask
            dist[...] = fold(distance * SCALE)
            coef_h[...] = fold(cut)
            coef_x[...] = fold(slope)
            coef_t[...] = fold(cut * TANGENT)
            inverse = 1.0 / distance
            for k in range(3):
                geom_out[0, k] = fold(separation[k] * inverse)
            geom_out[0, 3] = fold(slope)
            c_hi, c_lo = split2(cut)
            bias_part = (dot(c_hi, proj_t) + dot(c_lo, proj_t)) * b_f2[...]
            here = pl.ds(pl.multiple_of(row_tile * tile, tile), tile)
            msg[here, :] = msg[here, :] + bias_part

        centers = lax.broadcasted_iota(jnp.int32, (nbasis, 2 * tile), 0).astype(F32) * (
            SCALE * CENTER_MAX / (nbasis - 1)
        )
        shift = math.log2(LOG2E)
        ones = jnp.ones((16, 2 * tile), BF16)

        @pl.loop(0, CHUNK // 8)
        def _(group):
            base = pl.multiple_of(chunk * CHUNK + group * 8, 8)
            d8 = dist[pl.ds(base, 8), :]
            h8 = coef_h[pl.ds(base, 8), :]
            x8 = coef_x[pl.ds(base, 8), :]
            t8 = coef_t[pl.ds(base, 8), :]
            sums = []
            for u in range(8):
                offset = d8[u : u + 1] - centers
                gauss = jnp.exp2(shift - offset * offset)
                basis = jnp.concatenate(
                    [gauss.astype(BF16), (offset * gauss).astype(BF16), ones], axis=0
                )
                pre = dot(lhs[...], basis)
                total = 0.5 + jnp.exp2(pre[:hidden])
                value = jnp.log(total)
                slope = (2.0 - pl.reciprocal(total, approx=True)) * pre[hidden:]
                left = (h8[u : u + 1] * value).astype(BF16)
                tangents[0, group * 8 + u] = (
                    x8[u : u + 1] * value + t8[u : u + 1] * slope
                ).astype(BF16)
                mixed = dot(left, diag[...])
                sums.append(jnp.sum(mixed * w2[...], axis=0, keepdims=True))
            rows[pl.ds(base, 8), :] = jnp.concatenate(sums, axis=0)

        @pl.when(chunk == pl.num_programs(1) - 1)
        def _():
            here = pl.ds(pl.multiple_of(info[3 + slot] * tile, tile), tile)
            msg[here, :] = msg[here, :] + unfold(rows[...])


def force_kernel(
    n_row, tp, info, msg_a, msg_b, features, w_o1, b_o1, w_o2, b_o2, read_w, w_f2, b_f2, proj, geom, tangents,
    features_out, col_force, row_force,
    w2, grads, pre_act, diag, grad_rows, rows,
):
    slot, chunk = pl.program_id(0), pl.program_id(1)
    tile = features.shape[1]

    @pl.when((slot == 0) & (chunk == 0))
    def _():
        col_force[...] = jnp.zeros_like(col_force)
        row_force[...] = jnp.zeros_like(row_force)
        wide = w_f2[...].astype(F32)
        w2[...] = jnp.concatenate([wide, wide], axis=1)
        messages = (msg_a[...] + msg_b[...]).astype(BF16)
        pre = dot(messages, w_o1[...]) + b_o1[...]
        pre_act[...] = pre
        own = pre_act[pl.ds(pl.multiple_of(info[1] * tile, tile), tile), :]
        active = jnp.maximum(own, 0.0) + jnp.log(1.0 + jnp.exp(-jnp.abs(own))) - math.log(2.0)
        update = dot(active.astype(BF16), w_o2[...]) + b_o2[...]
        features_out[...] = (features[...].astype(F32) + update.T).astype(BF16)
        readout = jnp.broadcast_to(read_w[...], (8, tile))
        r_hi = readout.astype(BF16)
        rest = readout - r_hi.astype(F32)
        r_mid, r_lo = split2(rest)
        direction = (
            dot_t(r_hi, w_o2[...]) + (dot_t(r_mid, w_o2[...]) + dot_t(r_lo, w_o2[...]))
        )[0:1]
        s_hi, s_lo = split2(direction / (1.0 + jnp.exp(-pre)))
        grads[...] = dot_t(s_hi, w_o1[...]) + dot_t(s_lo, w_o1[...])

    @pl.when(slot < info[2])
    def _():
        @pl.when(chunk == 0)
        def _():
            here = pl.ds(pl.multiple_of(info[3 + slot] * tile, tile), tile)
            grad_rows[...] = fold(grads[here, :])
            diag[...] = block_diag(proj[0])

        @pl.loop(0, CHUNK // 8)
        def _(group):
            base = pl.multiple_of(chunk * CHUNK + group * 8, 8)
            g8 = grad_rows[pl.ds(base, 8), :]
            sums = []
            for u in range(8):
                left = (w2[...] * g8[u : u + 1]).astype(BF16)
                mixed = dot(left, diag[...])
                sums.append(
                    jnp.sum(mixed * tangents[0, group * 8 + u].astype(F32), axis=0, keepdims=True)
                )
            rows[pl.ds(base, 8), :] = jnp.concatenate(sums, axis=0)

        @pl.when(chunk == pl.num_programs(1) - 1)
        def _():
            row_tile, col_tile = info[3 + slot], info[3 + tp + slot]
            g_hi, g_lo = split2(unfold(grad_rows[...]) * b_f2[...])
            bias_part = dot(g_hi, proj[0]) + dot(g_lo, proj[0])
            dist_grad = unfold(rows[...]) + unfold(geom[0, 3]) * bias_part
            to_rows, to_cols = [], []
            for k in range(3):
                push = unfold(geom[0, k]) * dist_grad
                to_cols.append(jnp.sum(push, axis=0, keepdims=True))
                to_rows.append(-jnp.sum(push.T, axis=0, keepdims=True))
            zero = jnp.zeros((5, tile), F32)
            place = reverse_bits(col_tile ^ info[0], n_row)
            col_force[place] = col_force[place] + jnp.concatenate(to_cols + [zero], axis=0)
            n_col = row_force.shape[0]
            place = reverse_bits(row_tile ^ info[1], n_col)
            row_force[place] = row_force[place] + jnp.concatenate(to_rows + [zero], axis=0)


def exchange(value, axis, size, step):
    return lax.ppermute(value, axis, [(i, i ^ step) for i in range(size)])


def whole(shape):
    return pl.BlockSpec(shape, lambda s, c, info: (0,) * len(shape))


def local(
    features, positions, tile_pairs, pair_count, masks,
    w_in, w_f1, b_f1, w_f2, b_f2, w_o1, b_o1, w_o2, b_o2, read_w,
):
    n_feat, owned = features.shape
    tile = masks.shape[-1]
    tp = masks.shape[2]
    n_row = lax.axis_size("row")
    n_col = lax.axis_size("col")
    row_index = lax.axis_index("row")
    col_index = lax.axis_index("col")
    span = n_col * owned
    half = tile // 2
    chunks = half // CHUNK

    p_hi = lax.reduce_precision(positions, 8, 7)
    p_mid = lax.reduce_precision(positions - p_hi, 8, 7)
    p_lo = positions - p_hi - p_mid
    pieces = jnp.concatenate([p_hi, p_mid, p_lo, jnp.zeros((POS_ROWS - 9, owned), F32)], axis=0)
    near = jnp.concatenate([features, pieces.astype(BF16)], axis=0)[None]
    step = n_row // 2
    while step > 1:
        near = jnp.concatenate([near, exchange(near, "row", n_row, step)], axis=0)
        step //= 2
    far = exchange(near, "row", n_row, 1)
    col_pos = jnp.concatenate([positions, jnp.zeros((5, owned), F32)], axis=0)[None]
    step = 1
    while step < n_col:
        col_pos = jnp.concatenate([col_pos, exchange(col_pos, "col", n_col, step)], axis=0)
        step *= 2

    info = jnp.concatenate(
        [
            jnp.stack([row_index, col_index, pair_count[0, 0]]).astype(jnp.int32),
            tile_pairs[0, 0].reshape(-1),
        ]
    )

    def slot_of(s, info):
        return jnp.minimum(s, info[2] - 1)

    def chunk_of(s, c, info):
        return jnp.where(s < info[2], c, chunks - 1)

    tangent_spec = pl.BlockSpec(
        (1, CHUNK, n_feat, 2 * tile),
        lambda s, c, info: (slot_of(s, info), chunk_of(s, c, info), 0, 0),
    )
    proj_spec = pl.BlockSpec((1, n_feat, tile), lambda s, c, info: (slot_of(s, info), 0, 0))
    geom_spec = pl.BlockSpec((1, 4, half, 2 * tile), lambda s, c, info: (slot_of(s, info), 0, 0, 0))
    params = pltpu.CompilerParams(
        dimension_semantics=("arbitrary", "arbitrary"), vmem_limit_bytes=48 * 1024 * 1024
    )
    operands = (
        near, far, col_pos, masks[0, 0], w_in, w_f1, b_f1[None], w_f2, b_f2[None],
    )
    pair_plane = pltpu.VMEM((half, 2 * tile), F32)
    nbasis, hidden = w_f1.shape
    partial, tangents, proj, geom = pl.pallas_call(
        functools.partial(pair_kernel, n_row),
        grid_spec=pltpu.PrefetchScalarGridSpec(
            num_scalar_prefetch=1,
            grid=(tp, chunks),
            in_specs=[whole(x.shape) for x in operands],
            out_specs=[whole((span, n_feat)), tangent_spec, proj_spec, geom_spec],
            scratch_shapes=[
                pltpu.VMEM((2 * hidden, 2 * nbasis + 16), BF16),
                pltpu.VMEM((hidden, 2 * n_feat), F32),
                pltpu.VMEM((n_feat, n_feat), BF16),
                pltpu.VMEM((2 * tile, 2 * n_feat), BF16),
                pair_plane, pair_plane, pair_plane, pair_plane, pair_plane,
            ],
        ),
        out_shape=[
            jax.ShapeDtypeStruct((span, n_feat), F32),
            jax.ShapeDtypeStruct((tp, half, n_feat, 2 * tile), BF16),
            jax.ShapeDtypeStruct((tp, n_feat, tile), BF16),
            jax.ShapeDtypeStruct((tp, 4, half, 2 * tile), F32),
        ],
        compiler_params=params,
        name="pair_messages",
    )(info, *operands)

    step = 1
    while step < n_col // 2:
        partial = partial + exchange(partial, "col", n_col, step)
        step *= 2
    other = exchange(partial, "col", n_col, step)

    operands = (
        partial, other, features, w_o1, b_o1[None], w_o2, b_o2[None], read_w[None], w_f2, b_f2[None],
    )
    features_out, col_force, row_force = pl.pallas_call(
        functools.partial(force_kernel, n_row, tp),
        grid_spec=pltpu.PrefetchScalarGridSpec(
            num_scalar_prefetch=1,
            grid=(tp, chunks),
            in_specs=[whole(x.shape) for x in operands] + [proj_spec, geom_spec, tangent_spec],
            out_specs=[
                whole((n_feat, owned)),
                whole((n_row, 8, owned)),
                whole((n_col, 8, owned)),
            ],
            scratch_shapes=[
                pltpu.VMEM((hidden, 2 * n_feat), F32),
                pltpu.VMEM((span, n_feat), F32),
                pltpu.VMEM((span, n_feat), F32),
                pltpu.VMEM((2 * tile, 2 * n_feat), BF16),
                pair_plane, pair_plane,
            ],
        ),
        out_shape=[
            jax.ShapeDtypeStruct((n_feat, owned), BF16),
            jax.ShapeDtypeStruct((n_row, 8, owned), F32),
            jax.ShapeDtypeStruct((n_col, 8, owned), F32),
        ],
        compiler_params=params,
        name="pair_forces",
    )(info, *operands, proj, geom, tangents)

    def reduce_halves(total, axis, size):
        step = 1
        while step < size:
            keep = total.shape[0] // 2
            total = total[:keep] + exchange(total[keep:], axis, size, step)
            step *= 2
        return total[0]

    forces = reduce_halves(row_force, "col", n_col) + reduce_halves(col_force, "row", n_row)
    return (features_out, forces[:3])


def solution(mesh):
    atoms = P(None, ("row", "col"))
    in_specs = (
        atoms,
        atoms,
        P("row", "col", None, None),
        P("row", "col"),
        P("row", "col", None, None, None),
    ) + (P(),) * 10
    return jax.shard_map(
        local, mesh=mesh, in_specs=in_specs, out_specs=(atoms, atoms), check_vma=False
    )
```

time: 356 us -> 124 us (0.35)
  matrix products: 132 us -> 0 us
  blocking collectives: 97.2 us -> 0 us
  starting transfers between devices: 0.08 us -> 45.9 us
  waiting for transfers between devices: 64 us -> 23.7 us
  Pallas kernels: 0 us -> 39.4 us
  loops' own time: 17.9 us -> 0 us
  between operations: 14.2 us -> 1.36 us
  other arithmetic: 12.7 us -> 0.85 us
  local copies, waits for them, and re-layouts: 18 us -> 11.7 us
    dot_general x21 -> x0, matrix products: 132 us -> none  [the longest x8 71.3 us: filter_forward(): jnp.einsum('hf,hrc->frc', w_f2, hidden, preferred_element_type=jnp.float32)]
    all_gather x2 -> x0, blocking collectives: 88.9 us -> none  [the longest x1 70.2 us: local(): lax.all_gather(positions, ('row', 'col'), axis=1, tiled=True)]
    unnamed x4 -> x0, waiting for transfers between devices: 64 us -> none
    ppermute x0 -> x11, starting transfers between devices: none -> 45.9 us  [exchange(): return lax.ppermute(value, axis, [(i, i ^ step) for i in range(size)])]
    pallas_call x0 -> x2, Pallas kernels: none -> 39.4 us  [the longest x1 28.4 us: local(): pl.pallas_call(functools.partial(pair_kernel, n_row), grid_spec=pltpu.Pre...]
    ppermute x0 -> x11, waiting for transfers between devices: none -> 23.7 us  [exchange(): return lax.ppermute(value, axis, [(i, i ^ step) for i in range(size)])]
    another operation x2 -> x0, loops' own time: 17.9 us -> none  [the longest x1 9.31 us: local(): lax.fori_loop(jnp.int32(0), pair_total, backward_slot, (jnp.zeros((3, row...]
    dynamic_slice x34 -> x0, local copies, waits for them, and re-layouts: 12.1 us -> none  [the longest x8 11.4 us: locate(): col_start = slot_pairs[1, slot_index] * tile]
  transfers between devices with their start and end apart: 2 -> 11, of which waited for: 2 -> 9; matrix products, arithmetic and copies ran while one was open for 1% -> 1% of each run, Pallas kernels for 0% -> 0%
where the time goes in v1:
time: 124 us; the launch traced here: 123 us
  starting transfers between devices  45.9 us (37%)
  Pallas kernels  39.4 us (32%)
  waiting for transfers between devices  23.7 us (19%)
  local copies, waits for them, and re-layouts  11.7 us (9%)
  between operations  1.36 us (1%)
    ppermute x11, starting transfers between devices, exchange(): return lax.ppermute(value, axis, [(i, i ^ step) for i in range(size)])  45.9 us
    pallas_call x1, Pallas kernels, local(): pl.pallas_call(functools.partial(pair_kernel, n_row), grid_spec=pltpu.Pre...  28.4 us
    ppermute x11, waiting for transfers between devices, exchange(): return lax.ppermute(value, axis, [(i, i ^ step) for i in range(size)])  23.7 us
    pallas_call x1, Pallas kernels, local(): pl.pallas_call(functools.partial(force_kernel, n_row, tp), grid_spec=pltp...  11 us
    unnamed x24, local copies, waits for them, and re-layouts  8.73 us
  transfers between devices with their start and end apart: 11, of which 9 were waited for; matrix products, arithmetic and copies ran while one was open for 1% of the time, Pallas kernels for 0%

profile of v1, /device:TPU:0, one launch (start us, length us, event | category | flops | bytes accessed | tf_op | source)
XLA Modules:
  0.0 122.9 jit_solution(11944009995997945950)
XLA Ops:
  0.6 0.7 fusion.1
  1.3 0.9 concatenate.27
  2.2 4.1 %collective-permute-start = (bf16[1,144,128]{2,1,0:T(8,128)(2,1)S(1)}, bf16[1,144,128]{2,1,0:T(8,128)(2,1)S(1)}, u32[]{:S(2)}, u32[]{:S(2)}) collective-permute-start(bf16[1,144,128]{2,1,0:T(8,128)(2,1)S(1)} %bitcast.22), channel_id=1, source_target_pairs={{0,16},{2,18},{4,20},{6,22},{8,24},{10,26},{12,28},{14,30},{16,0},... | collective-permute-start | bytes 110600 | tf_op jit(solution)/shard_map/ppermute | solution.py:247
  6.3 2.3 %collective-permute-done = bf16[1,144,128]{2,1,0:T(8,128)(2,1)S(1)} collective-permute-done((bf16[1,144,128]{2,1,0:T(8,128)(2,1)S(1)}, bf16[1,144,128]{2,1,0:T(8,128)(2,1)S(1)}, u32[]{:S(2)}, u32[]{:S(2)}) %collective-permute-start) | collective-permute-done | bytes 36896 | tf_op jit(solution)/shard_map/ppermute | solution.py:247
  8.7 1.6 %collective-permute-start.1 = (bf16[2,144,128]{2,1,0:T(8,128)(2,1)S(1)}, bf16[2,144,128]{2,1,0:T(8,128)(2,1)S(1)}, u32[]{:S(2)}, u32[]{:S(2)}) collective-permute-start(bf16[2,144,128]{2,1,0:T(8,128)(2,1)S(1)} %pad_maximum_fusion.2), channel_id=1, source_target_pairs={{0,8},{2,10},{4,12},{6,14},{8,0},{10,2},{12,4},{14,6},{16,24},{18,... | collective-permute-start | bytes 221192 | tf_op jit(solution)/shard_map/ppermute | solution.py:247
  10.2 2.8 %collective-permute-done.1 = bf16[2,144,128]{2,1,0:T(8,128)(2,1)S(1)} collective-permute-done((bf16[2,144,128]{2,1,0:T(8,128)(2,1)S(1)}, bf16[2,144,128]{2,1,0:T(8,128)(2,1)S(1)}, u32[]{:S(2)}, u32[]{:S(2)}) %collective-permute-start.1) | collective-permute-done | bytes 73760 | tf_op jit(solution)/shard_map/ppermute | solution.py:247
  13.1 1.8 %collective-permute-start.2 = (bf16[4,144,128]{2,1,0:T(8,128)(2,1)S(1)}, bf16[4,144,128]{2,1,0:T(8,128)(2,1)S(1)}, u32[]{:S(2)}, u32[]{:S(2)}) collective-permute-start(bf16[4,144,128]{2,1,0:T(8,128)(2,1)S(1)} %pad_maximum_fusion.1), channel_id=1, source_target_pairs={{0,4},{2,6},{4,0},{6,2},{8,12},{10,14},{12,8},{14,10},{16,20},{18,... | collective-permute-start | bytes 442376 | tf_op jit(solution)/shard_map/ppermute | solution.py:247
  14.9 3.4 %collective-permute-done.2 = bf16[4,144,128]{2,1,0:T(8,128)(2,1)S(1)} collective-permute-done((bf16[4,144,128]{2,1,0:T(8,128)(2,1)S(1)}, bf16[4,144,128]{2,1,0:T(8,128)(2,1)S(1)}, u32[]{:S(2)}, u32[]{:S(2)}) %collective-permute-start.2) | collective-permute-done | bytes 147488 | tf_op jit(solution)/shard_map/ppermute | solution.py:247
  18.3 0.1 collective-permute-start.3
  18.4 0.7 pad_bitcast_fusion
  19.1 1.7 %collective-permute-start.4 = (f32[1,8,128]{2,1,0:T(8,128)S(1)}, f32[1,8,128]{2,1,0:T(8,128)S(1)}, u32[]{:S(2)}, u32[]{:S(2)}) collective-permute-start(f32[1,8,128]{2,1,0:T(8,128)S(1)} %pad_bitcast_fusion), channel_id=1, source_target_pairs={{0,1},{1,0},{2,3},{3,2},{4,5},{5,4},{6,7},{7,6},{8,9},{9,8},{10,11... | collective-permute-start | bytes 12296 | tf_op jit(solution)/shard_map/ppermute | solution.py:247
  21.5 0.8 reshape_squeeze.3
  22.2 0.1 pad_add_fusion.info
  22.3 0.4 collective-permute-done.4
  22.7 0.0 collective-permute-done.3.far
  22.7 0.0 copy-start
  22.7 0.9 copy-done
  23.7 0.0 copy-start.1
  23.7 0.8 copy-done.1
  24.4 0.0 copy-start.5
  24.4 0.8 copy-done.5
  25.2 0.0 copy-start.6
  25.2 0.7 copy-done.6
  25.9 0.0 copy-start.7
  25.9 0.7 copy-done.7
  26.6 0.0 copy-start.8
  26.6 0.7 copy-done.8
  27.2 28.4 %pair_messages.1 = (f32[256,128]{1,0:T(8,128)S(1)}, bf16[4,64,128,256]{3,2,1,0:T(8,128)(2,1)}, bf16[4,128,128]{2,1,0:T(8,128)(2,1)S(1)}, f32[4,4,64,256]{3,2,1,0:T(8,128)S(1)}) custom-call(s32[11]{0:T(128)S(1)} %pad_add_fusion.info, bf16[8,144,128]{2,1,0:T(8,128)(2,1)S(1)} %pad_maximum_fusion.near, bf16[8,144,128]{2,1,0:T(8,128)(2,1)S(1)} %collective-permute-done.3.far, ...), custom_call_target="tpu_custom_call" | custom-call | tf_op jit(solution)/shard_map/pair_messages/pallas_call | solution.py:312
  55.6 0.0 collective-permute-start.5
  55.7 5.0 %collective-permute-done.5.msg_b = f32[256,128]{1,0:T(8,128)S(1)} collective-permute-done((f32[256,128]{1,0:T(8,128)S(1)}, f32[256,128]{1,0:T(8,128)S(1)}, u32[]{:S(2)}, u32[]{:S(2)}) %collective-permute-start.5) | collective-permute-done | bytes 131104 | tf_op jit(solution)/shard_map/ppermute | solution.py:247
  60.6 0.8 copy-done.2
  61.4 0.8 copy-done.3
  62.1 0.8 copy-done.4
  62.9 0.7 copy-done.9
  63.5 0.7 copy-done.10
  64.2 0.7 copy-done.11
  64.9 11.0 %pair_forces.1 = (bf16[128,128]{1,0:T(8,128)(2,1)}, f32[16,8,128]{2,1,0:T(8,128)S(1)}, f32[2,8,128]{2,1,0:T(8,128)S(1)}) custom-call(s32[11]{0:T(128)S(1)} %pad_add_fusion.info, f32[256,128]{1,0:T(8,128)S(1)} %get-tuple-element.9.msg_a, f32[256,128]{1,0:T(8,128)S(1)} %collective-permute-done.5.msg_b, bf16[128,128]{1,0:T(8,128)(2,1)S(1)} %copy-done.2, ...), custom_call_target="tpu_custom_call" | custom-call | tf_op jit(solution)/shard_map/pair_forces/pallas_call | solution.py:346
  75.8 32.3 %collective-permute-start.7 = (f32[8,8,128]{2,1,0:T(8,128)S(1)}, f32[8,8,128]{2,1,0:T(8,128)S(1)}, u32[]{:S(2)}, u32[]{:S(2)}) collective-permute-start(f32[8,8,128]{2,1,0:T(8,128)S(1)} %slice.39), channel_id=1, source_target_pairs={{0,2},{2,0},{4,6},{6,4},{8,10},{10,8},{12,14},{14,12},{16,18},{18,... | collective-permute-start | bytes 98312 | tf_op jit(solution)/shard_map/ppermute | solution.py:247
  108.1 0.9 collective-permute-done.7
  109.0 0.1 collective-permute-start.8
  109.0 3.7 %collective-permute-done.8 = f32[4,8,128]{2,1,0:T(8,128)S(1)} collective-permute-done((f32[4,8,128]{2,1,0:T(8,128)S(1)}, f32[4,8,128]{2,1,0:T(8,128)S(1)}, u32[]{:S(2)}, u32[]{:S(2)}) %collective-permute-start.8) | collective-permute-done | bytes 16416 | tf_op jit(solution)/shard_map/ppermute | solution.py:247
  112.8 0.0 collective-permute-start.9
  112.8 0.1 collective-permute-start.6
  112.9 3.6 %collective-permute-done.9 = f32[2,8,128]{2,1,0:T(8,128)S(1)} collective-permute-done((f32[2,8,128]{2,1,0:T(8,128)S(1)}, f32[2,8,128]{2,1,0:T(8,128)S(1)}, u32[]{:S(2)}, u32[]{:S(2)}) %collective-permute-start.9) | collective-permute-done | bytes 8224 | tf_op jit(solution)/shard_map/ppermute | solution.py:247
  116.4 4.3 %collective-permute-start.10 = (f32[1,8,128]{2,1,0:T(8,128)S(1)}, f32[1,8,128]{2,1,0:T(8,128)S(1)}, u32[]{:S(2)}, u32[]{:S(2)}) collective-permute-start(f32[1,8,128]{2,1,0:T(8,128)S(1)} %slice.53), channel_id=1, source_target_pairs={{0,16},{2,18},{4,20},{6,22},{8,24},{10,26},{12,28},{14,30},{16,0},... | collective-permute-start | bytes 12296 | tf_op jit(solution)/shard_map/ppermute | solution.py:247
  120.7 0.0 collective-permute-done.6
  120.7 1.6 %collective-permute-done.10 = f32[1,8,128]{2,1,0:T(8,128)S(1)} collective-permute-done((f32[1,8,128]{2,1,0:T(8,128)S(1)}, f32[1,8,128]{2,1,0:T(8,128)S(1)}, u32[]{:S(2)}, u32[]{:S(2)}) %collective-permute-start.10) | collective-permute-done | bytes 4128 | tf_op jit(solution)/shard_map/ppermute | solution.py:247
  122.3 0.6 slice_bitcast_fusion
  (20 shorter events, 0.1 us)
Async XLA Ops:
  2.2 6.4 %collective-permute-start = (bf16[1,144,128]{2,1,0:T(8,128)(2,1)S(1)}, bf16[1,144,128]{2,1,0:T(8,128)(2,1)S(1)}, u32[]{:S(2)}, u32[]{:S(2)}) collective-permute-start(bf16[1,144,128]{2,1,0:T(8,128)(2,1)S(1)} %bitcast.22), channel_id=1, source_target_pairs={{0,16},{2,18},{4,20},{6,22},{8,24},{10,26},{12,28},{14,30},{16,0},... | collective-permute-start | bytes 110600 | tf_op jit(solution)/shard_map/ppermute | solution.py:247
  8.7 4.4 %collective-permute-start.1 = (bf16[2,144,128]{2,1,0:T(8,128)(2,1)S(1)}, bf16[2,144,128]{2,1,0:T(8,128)(2,1)S(1)}, u32[]{:S(2)}, u32[]{:S(2)}) collective-permute-start(bf16[2,144,128]{2,1,0:T(8,128)(2,1)S(1)} %pad_maximum_fusion.2), channel_id=1, source_target_pairs={{0,8},{2,10},{4,12},{6,14},{8,0},{10,2},{12,4},{14,6},{16,24},{18,... | collective-permute-start | bytes 221192 | tf_op jit(solution)/shard_map/ppermute | solution.py:247
  13.1 5.2 %collective-permute-start.2 = (bf16[4,144,128]{2,1,0:T(8,128)(2,1)S(1)}, bf16[4,144,128]{2,1,0:T(8,128)(2,1)S(1)}, u32[]{:S(2)}, u32[]{:S(2)}) collective-permute-start(bf16[4,144,128]{2,1,0:T(8,128)(2,1)S(1)} %pad_maximum_fusion.1), channel_id=1, source_target_pairs={{0,4},{2,6},{4,0},{6,2},{8,12},{10,14},{12,8},{14,10},{16,20},{18,... | collective-permute-start | bytes 442376 | tf_op jit(solution)/shard_map/ppermute | solution.py:247
  18.3 4.4 %collective-permute-start.3 = (bf16[8,144,128]{2,1,0:T(8,128)(2,1)S(1)}, bf16[8,144,128]{2,1,0:T(8,128)(2,1)S(1)}, u32[]{:S(2)}, u32[]{:S(2)}) collective-permute-start(bf16[8,144,128]{2,1,0:T(8,128)(2,1)S(1)} %pad_maximum_fusion.near), channel_id=1, source_target_pairs={{0,2},{2,0},{4,6},{6,4},{8,10},{10,8},{12,14},{14,12},{16,18},{18,... | collective-permute-start | bytes 884744 | tf_op jit(solution)/shard_map/ppermute | solution.py:247
  19.1 3.6 %collective-permute-start.4 = (f32[1,8,128]{2,1,0:T(8,128)S(1)}, f32[1,8,128]{2,1,0:T(8,128)S(1)}, u32[]{:S(2)}, u32[]{:S(2)}) collective-permute-start(f32[1,8,128]{2,1,0:T(8,128)S(1)} %pad_bitcast_fusion), channel_id=1, source_target_pairs={{0,1},{1,0},{2,3},{3,2},{4,5},{5,4},{6,7},{7,6},{8,9},{9,8},{10,11... | collective-permute-start | bytes 12296 | tf_op jit(solution)/shard_map/ppermute | solution.py:247
  22.7 1.0 copy-start
  23.7 0.8 copy-start.1
  24.4 0.8 copy-start.5
  25.2 0.7 copy-start.6
  25.9 0.7 copy-start.7
  26.6 0.7 copy-start.8
  55.6 5.0 %collective-permute-start.5 = (f32[256,128]{1,0:T(8,128)S(1)}, f32[256,128]{1,0:T(8,128)S(1)}, u32[]{:S(2)}, u32[]{:S(2)}) collective-permute-start(f32[256,128]{1,0:T(8,128)S(1)} %get-tuple-element.9.msg_a), channel_id=1, source_target_pairs={{0,1},{1,0},{2,3},{3,2},{4,5},{5,4},{6,7},{7,6},{8,9},{9,8},{10,11... | collective-permute-start | bytes 393224 | tf_op jit(solution)/shard_map/ppermute | solution.py:247
  60.6 0.8 copy-start.2
  61.4 0.8 copy-start.3
  62.1 0.8 copy-start.4
  62.9 0.7 copy-start.9
  63.5 0.7 copy-start.10
  64.2 0.7 copy-start.11
  75.8 33.1 %collective-permute-start.7 = (f32[8,8,128]{2,1,0:T(8,128)S(1)}, f32[8,8,128]{2,1,0:T(8,128)S(1)}, u32[]{:S(2)}, u32[]{:S(2)}) collective-permute-start(f32[8,8,128]{2,1,0:T(8,128)S(1)} %slice.39), channel_id=1, source_target_pairs={{0,2},{2,0},{4,6},{6,4},{8,10},{10,8},{12,14},{14,12},{16,18},{18,... | collective-permute-start | bytes 98312 | tf_op jit(solution)/shard_map/ppermute | solution.py:247
  109.0 3.8 %collective-permute-start.8 = (f32[4,8,128]{2,1,0:T(8,128)S(1)}, f32[4,8,128]{2,1,0:T(8,128)S(1)}, u32[]{:S(2)}, u32[]{:S(2)}) collective-permute-start(f32[4,8,128]{2,1,0:T(8,128)S(1)} %slice.49), channel_id=1, source_target_pairs={{0,4},{2,6},{4,0},{6,2},{8,12},{10,14},{12,8},{14,10},{16,20},{18,... | collective-permute-start | bytes 49160 | tf_op jit(solution)/shard_map/ppermute | solution.py:247
  112.8 3.7 %collective-permute-start.9 = (f32[2,8,128]{2,1,0:T(8,128)S(1)}, f32[2,8,128]{2,1,0:T(8,128)S(1)}, u32[]{:S(2)}, u32[]{:S(2)}) collective-permute-start(f32[2,8,128]{2,1,0:T(8,128)S(1)} %slice.51), channel_id=1, source_target_pairs={{0,8},{2,10},{4,12},{6,14},{8,0},{10,2},{12,4},{14,6},{16,24},{18,... | collective-permute-start | bytes 24584 | tf_op jit(solution)/shard_map/ppermute | solution.py:247
  112.8 7.9 %collective-permute-start.6 = (f32[1,8,128]{2,1,0:T(8,128)S(1)}, f32[1,8,128]{2,1,0:T(8,128)S(1)}, u32[]{:S(2)}, u32[]{:S(2)}) collective-permute-start(f32[1,8,128]{2,1,0:T(8,128)S(1)} %slice.37), channel_id=1, source_target_pairs={{0,1},{1,0},{2,3},{3,2},{4,5},{5,4},{6,7},{7,6},{8,9},{9,8},{10,11... | collective-permute-start | bytes 12296 | tf_op jit(solution)/shard_map/ppermute | solution.py:247
  116.4 5.9 %collective-permute-start.10 = (f32[1,8,128]{2,1,0:T(8,128)S(1)}, f32[1,8,128]{2,1,0:T(8,128)S(1)}, u32[]{:S(2)}, u32[]{:S(2)}) collective-permute-start(f32[1,8,128]{2,1,0:T(8,128)S(1)} %slice.53), channel_id=1, source_target_pairs={{0,16},{2,18},{4,20},{6,22},{8,24},{10,26},{12,28},{14,30},{16,0},... | collective-permute-start | bytes 12296 | tf_op jit(solution)/shard_map/ppermute | solution.py:247

commit v2 on v1

--- a/solution.py
+++ b/solution.py
@@ -12,9 +12,9 @@
 GAMMA_RBF = 10.0
 CENTER_MAX = 10.0
 CUTOFF = 12.0
-LOG2E = math.log2(math.e)
-SCALE = math.sqrt(GAMMA_RBF * LOG2E)
-TANGENT = -GAMMA_RBF / (SCALE * LOG2E)
+LN2 = math.log(2.0)
+SCALE = math.sqrt(GAMMA_RBF / LN2)
+TANGENT = -GAMMA_RBF / SCALE
 POS_ROWS = 16
 CHUNK = 16
 F32 = jnp.float32
@@ -62,7 +62,7 @@
 def pair_kernel(
     n_row, info, near, far, col_pos, masks, w_in, w_f1, b_f1, w_f2, b_f2,
     msg, tangents, proj_out, geom_out,
-    lhs, w2, w_in_t, diag, dist, coef_h, coef_x, coef_t, rows,
+    lhs, w2, w_in_t, diag, dist, coef_h, coef_x, rows, left,
 ):
     slot, chunk = pl.program_id(0), pl.program_id(1)
     nbasis = w_f1.shape[0]
@@ -74,14 +74,14 @@
     def _():
         weights = w_f1[...].astype(F32)
         zero = jnp.zeros_like(weights)
-        bias = b_f1[...] * LOG2E - 1.0
+        bias = b_f1[...] * 0.5
         b_hi = bias.astype(BF16).astype(F32)
         b_mid = (bias - b_hi).astype(BF16).astype(F32)
         b_lo = bias - b_hi - b_mid
         extra = jnp.concatenate([b_hi, b_mid, b_lo, jnp.zeros((13, hidden), F32)], axis=0)
         table = jnp.concatenate(
             [
-                jnp.concatenate([weights, zero], axis=1),
+                jnp.concatenate([0.5 * weights, zero], axis=1),
                 jnp.concatenate([zero, weights], axis=1),
                 jnp.concatenate([extra, jnp.zeros_like(extra)], axis=1),
                 jnp.zeros((256 - 2 * nbasis - 16, 2 * hidden), F32),
@@ -122,9 +122,11 @@
             cut = 0.5 * (jnp.cos(angle) + 1.0) * mask
             slope = (-0.5 * math.pi / CUTOFF) * jnp.sin(angle) * mask
             dist[...] = fold(distance * SCALE)
-            coef_h[...] = fold(cut)
-            coef_x[...] = fold(slope)
-            coef_t[...] = fold(cut * TANGENT)
+            coef_h[...] = fold(-LN2 * cut)
+            coef_x[...] = fold(
+                jnp.sin(angle) / (jnp.cos(angle) + 1.0) * (LN2 * math.pi / CUTOFF / TANGENT)
+            )
+            geom_out[0, 4] = fold(cut * TANGENT)
             inverse = 1.0 / distance
             for k in range(3):
                 geom_out[0, k] = fold(separation[k] * inverse)
@@ -137,34 +139,28 @@
         centers = lax.broadcasted_iota(jnp.int32, (nbasis, 2 * tile), 0).astype(F32) * (
             SCALE * CENTER_MAX / (nbasis - 1)
         )
-        shift = math.log2(LOG2E)
         ones = jnp.ones((16, 2 * tile), BF16)
-
-        @pl.loop(0, CHUNK // 8)
-        def _(group):
-            base = pl.multiple_of(chunk * CHUNK + group * 8, 8)
-            d8 = dist[pl.ds(base, 8), :]
-            h8 = coef_h[pl.ds(base, 8), :]
-            x8 = coef_x[pl.ds(base, 8), :]
-            t8 = coef_t[pl.ds(base, 8), :]
-            sums = []
-            for u in range(8):
-                offset = d8[u : u + 1] - centers
-                gauss = jnp.exp2(shift - offset * offset)
-                basis = jnp.concatenate(
-                    [gauss.astype(BF16), (offset * gauss).astype(BF16), ones], axis=0
-                )
-                pre = dot(lhs[...], basis)
-                total = 0.5 + jnp.exp2(pre[:hidden])
-                value = jnp.log(total)
-                slope = (2.0 - pl.reciprocal(total, approx=True)) * pre[hidden:]
-                left = (h8[u : u + 1] * value).astype(BF16)
-                tangents[0, group * 8 + u] = (
-                    x8[u : u + 1] * value + t8[u : u + 1] * slope
-                ).astype(BF16)
-                mixed = dot(left, diag[...])
-                sums.append(jnp.sum(mixed * w2[...], axis=0, keepdims=True))
-            rows[pl.ds(base, 8), :] = jnp.concatenate(sums, axis=0)
+        base = pl.multiple_of(chunk * CHUNK, CHUNK)
+        here = pl.ds(base, CHUNK)
+        d, h, x = dist[here, :], coef_h[here, :], coef_x[here, :]
+        for u in range(CHUNK):
+            offset = d[u : u + 1] - centers
+            gauss = jnp.exp2(-(offset * offset))
+            basis = jnp.concatenate(
+                [gauss.astype(BF16), (offset * gauss).astype(BF16), ones], axis=0
+            )
+            pre = dot(lhs[...], basis)
+            bend = jnp.tanh(pre[:hidden])
+            value = lax.log2(1.0 - bend)
+            slope = (1.0 + bend) * pre[hidden:]
+            left[pl.ds(u * hidden, hidden), :] = (h[u : u + 1] * value).astype(BF16)
+            tangents[0, u] = (x[u : u + 1] * value + slope).astype(BF16)
+        mixed = dot(left[...], diag[...])
+        sums = [
+            jnp.sum(mixed[u * hidden : (u + 1) * hidden] * w2[...], axis=0, keepdims=True)
+            for u in range(CHUNK)
+        ]
+        rows[here, :] = jnp.concatenate(sums, axis=0)
 
         @pl.when(chunk == pl.num_programs(1) - 1)
         def _():
@@ -175,7 +171,7 @@
 def force_kernel(
     n_row, tp, info, msg_a, msg_b, features, w_o1, b_o1, w_o2, b_o2, read_w, w_f2, b_f2, proj, geom, tangents,
     features_out, col_force, row_force,
-    w2, grads, pre_act, diag, grad_rows, rows,
+    w2, grads, pre_act, diag, grad_rows, rows, left,
 ):
     slot, chunk = pl.program_id(0), pl.program_id(1)
     tile = features.shape[1]
@@ -211,25 +207,28 @@
             grad_rows[...] = fold(grads[here, :])
             diag[...] = block_diag(proj[0])
 
-        @pl.loop(0, CHUNK // 8)
-        def _(group):
-            base = pl.multiple_of(chunk * CHUNK + group * 8, 8)
-            g8 = grad_rows[pl.ds(base, 8), :]
-            sums = []
-            for u in range(8):
-                left = (w2[...] * g8[u : u + 1]).astype(BF16)
-                mixed = dot(left, diag[...])
-                sums.append(
-                    jnp.sum(mixed * tangents[0, group * 8 + u].astype(F32), axis=0, keepdims=True)
-                )
-            rows[pl.ds(base, 8), :] = jnp.concatenate(sums, axis=0)
+        here = pl.ds(pl.multiple_of(chunk * CHUNK, CHUNK), CHUNK)
+        g = grad_rows[here, :]
+        hidden = w2.shape[0]
+        for u in range(CHUNK):
+            left[pl.ds(u * hidden, hidden), :] = (w2[...] * g[u : u + 1]).astype(BF16)
+        mixed = dot(left[...], diag[...])
+        sums = [
+            jnp.sum(
+                mixed[u * hidden : (u + 1) * hidden] * tangents[0, u].astype(F32),
+                axis=0,
+                keepdims=True,
+            )
+            for u in range(CHUNK)
+        ]
+        rows[here, :] = jnp.concatenate(sums, axis=0)
 
         @pl.when(chunk == pl.num_programs(1) - 1)
         def _():
             row_tile, col_tile = info[3 + slot], info[3 + tp + slot]
             g_hi, g_lo = split2(unfold(grad_rows[...]) * b_f2[...])
             bias_part = dot(g_hi, proj[0]) + dot(g_lo, proj[0])
-            dist_grad = unfold(rows[...]) + unfold(geom[0, 3]) * bias_part
+            dist_grad = unfold(geom[0, 4] * rows[...]) + unfold(geom[0, 3]) * bias_part
             to_rows, to_cols = [], []
             for k in range(3):
                 push = unfold(geom[0, k]) * dist_grad
@@ -300,9 +299,9 @@
         lambda s, c, info: (slot_of(s, info), chunk_of(s, c, info), 0, 0),
     )
     proj_spec = pl.BlockSpec((1, n_feat, tile), lambda s, c, info: (slot_of(s, info), 0, 0))
-    geom_spec = pl.BlockSpec((1, 4, half, 2 * tile), lambda s, c, info: (slot_of(s, info), 0, 0, 0))
+    geom_spec = pl.BlockSpec((1, 5, half, 2 * tile), lambda s, c, info: (slot_of(s, info), 0, 0, 0))
     params = pltpu.CompilerParams(
-        dimension_semantics=("arbitrary", "arbitrary"), vmem_limit_bytes=48 * 1024 * 1024
+        dimension_semantics=("arbitrary", "arbitrary"), vmem_limit_bytes=60 * 1024 * 1024
     )
     operands = (
         near, far, col_pos, masks[0, 0], w_in, w_f1, b_f1[None], w_f2, b_f2[None],
@@ -321,14 +320,15 @@
                 pltpu.VMEM((hidden, 2 * n_feat), F32),
                 pltpu.VMEM((n_feat, n_feat), BF16),
                 pltpu.VMEM((2 * tile, 2 * n_feat), BF16),
-                pair_plane, pair_plane, pair_plane, pair_plane, pair_plane,
+                pair_plane, pair_plane, pair_plane, pair_plane,
+                pltpu.VMEM((CHUNK * hidden, 2 * tile), BF16),
             ],
         ),
         out_shape=[
             jax.ShapeDtypeStruct((span, n_feat), F32),
             jax.ShapeDtypeStruct((tp, half, n_feat, 2 * tile), BF16),
             jax.ShapeDtypeStruct((tp, n_feat, tile), BF16),
-            jax.ShapeDtypeStruct((tp, 4, half, 2 * tile), F32),
+            jax.ShapeDtypeStruct((tp, 5, half, 2 * tile), F32),
         ],
         compiler_params=params,
         name="pair_messages",
@@ -360,6 +360,7 @@
                 pltpu.VMEM((span, n_feat), F32),
                 pltpu.VMEM((2 * tile, 2 * n_feat), BF16),
                 pair_plane, pair_plane,
+                pltpu.VMEM((CHUNK * hidden, 2 * n_feat), BF16),
             ],
         ),
         out_shape=[

time: 124 us -> 92.9 us (0.75)
  Pallas kernels: 39.4 us -> 27.8 us
  starting transfers between devices: 45.9 us -> 37 us
  waiting for transfers between devices: 23.7 us -> 16.5 us
  local copies, waits for them, and re-layouts: 11.7 us -> 5.76 us
  other arithmetic: 0.85 us -> 3.48 us
    pallas_call x1, Pallas kernels: 28.4 us -> 16.6 us  [local(): pl.pallas_call(functools.partial(pair_kernel, n_row), grid_spec=pltpu.Pre...]
    ppermute x11, starting transfers between devices: 45.9 us -> 37 us  [exchange(): return lax.ppermute(value, axis, [(i, i ^ step) for i in range(size)])]
    unnamed x24 -> x6, local copies, waits for them, and re-layouts: 8.73 us -> 1.36 us
    ppermute x11, waiting for transfers between devices: 23.7 us -> 16.5 us  [exchange(): return lax.ppermute(value, axis, [(i, i ^ step) for i in range(size)])]
    slice x5, local copies, waits for them, and re-layouts: 0.02 us -> 1.45 us  [reduce_halves(): total = total[:keep] + exchange(total[keep:], axis, size, step)]
  transfers between devices with their start and end apart: 11 -> 11, of which waited for: 9 -> 8; matrix products, arithmetic and copies ran while one was open for 1% -> 4% of each run, Pallas kernels for 0% -> 0%
where the time goes in v2:
time: 92.9 us; the launch traced here: 91.9 us
  starting transfers between devices  37 us (40%)
  Pallas kernels  27.8 us (30%)
  waiting for transfers between devices  16.5 us (18%)
  local copies, waits for them, and re-layouts  5.76 us (6%)
  other arithmetic  3.48 us (4%)
  between operations  1.33 us (1%)
    ppermute x11, starting transfers between devices, exchange(): return lax.ppermute(value, axis, [(i, i ^ step) for i in range(size)])  37 us
    pallas_call x1, Pallas kernels, local(): pl.pallas_call(functools.partial(pair_kernel, n_row), grid_spec=pltpu.Pre...  16.6 us
    ppermute x11, waiting for transfers between devices, exchange(): return lax.ppermute(value, axis, [(i, i ^ step) for i in range(size)])  16.5 us
    pallas_call x1, Pallas kernels, local(): pl.pallas_call(functools.partial(force_kernel, n_row, tp), grid_spec=pltp...  11.2 us
  transfers between devices with their start and end apart: 11, of which 8 were waited for; matrix products, arithmetic and copies ran while one was open for 4% of the time, Pallas kernels for 0%

profile of v2, /device:TPU:0, one launch (start us, length us, event | category | flops | bytes accessed | tf_op | source)
XLA Modules:
  0.0 91.9 jit_solution(17703942756957484699)
XLA Ops:
  0.6 0.7 fusion.1
  1.3 0.9 concatenate.27
  2.2 4.1 %collective-permute-start = (bf16[1,144,128]{2,1,0:T(8,128)(2,1)S(1)}, bf16[1,144,128]{2,1,0:T(8,128)(2,1)S(1)}, u32[]{:S(2)}, u32[]{:S(2)}) collective-permute-start(bf16[1,144,128]{2,1,0:T(8,128)(2,1)S(1)} %bitcast.15), channel_id=1, source_target_pairs={{0,16},{2,18},{4,20},{6,22},{8,24},{10,26},{12,28},{14,30},{16,0},... | collective-permute-start | bytes 110600 | tf_op jit(solution)/shard_map/ppermute | solution.py:246
  6.3 2.3 %collective-permute-done = bf16[1,144,128]{2,1,0:T(8,128)(2,1)S(1)} collective-permute-done((bf16[1,144,128]{2,1,0:T(8,128)(2,1)S(1)}, bf16[1,144,128]{2,1,0:T(8,128)(2,1)S(1)}, u32[]{:S(2)}, u32[]{:S(2)}) %collective-permute-start) | collective-permute-done | bytes 36896 | tf_op jit(solution)/shard_map/ppermute | solution.py:246
  8.7 1.6 %collective-permute-start.1 = (bf16[2,144,128]{2,1,0:T(8,128)(2,1)S(1)}, bf16[2,144,128]{2,1,0:T(8,128)(2,1)S(1)}, u32[]{:S(2)}, u32[]{:S(2)}) collective-permute-start(bf16[2,144,128]{2,1,0:T(8,128)(2,1)S(1)} %pad_maximum_fusion.2), channel_id=1, source_target_pairs={{0,8},{2,10},{4,12},{6,14},{8,0},{10,2},{12,4},{14,6},{16,24},{18,... | collective-permute-start | bytes 221192 | tf_op jit(solution)/shard_map/ppermute | solution.py:246
  10.2 2.8 %collective-permute-done.1 = bf16[2,144,128]{2,1,0:T(8,128)(2,1)S(1)} collective-permute-done((bf16[2,144,128]{2,1,0:T(8,128)(2,1)S(1)}, bf16[2,144,128]{2,1,0:T(8,128)(2,1)S(1)}, u32[]{:S(2)}, u32[]{:S(2)}) %collective-permute-start.1) | collective-permute-done | bytes 73760 | tf_op jit(solution)/shard_map/ppermute | solution.py:246
  13.1 1.8 %collective-permute-start.2 = (bf16[4,144,128]{2,1,0:T(8,128)(2,1)S(1)}, bf16[4,144,128]{2,1,0:T(8,128)(2,1)S(1)}, u32[]{:S(2)}, u32[]{:S(2)}) collective-permute-start(bf16[4,144,128]{2,1,0:T(8,128)(2,1)S(1)} %pad_maximum_fusion.1), channel_id=1, source_target_pairs={{0,4},{2,6},{4,0},{6,2},{8,12},{10,14},{12,8},{14,10},{16,20},{18,... | collective-permute-start | bytes 442376 | tf_op jit(solution)/shard_map/ppermute | solution.py:246
  14.9 3.4 %collective-permute-done.2 = bf16[4,144,128]{2,1,0:T(8,128)(2,1)S(1)} collective-permute-done((bf16[4,144,128]{2,1,0:T(8,128)(2,1)S(1)}, bf16[4,144,128]{2,1,0:T(8,128)(2,1)S(1)}, u32[]{:S(2)}, u32[]{:S(2)}) %collective-permute-start.2) | collective-permute-done | bytes 147488 | tf_op jit(solution)/shard_map/ppermute | solution.py:246
  18.3 0.0 copy-start
  18.3 0.1 collective-permute-start.3
  18.4 0.7 pad_bitcast_fusion
  19.1 1.7 %collective-permute-start.4 = (f32[1,8,128]{2,1,0:T(8,128)S(1)}, f32[1,8,128]{2,1,0:T(8,128)S(1)}, u32[]{:S(2)}, u32[]{:S(2)}) collective-permute-start(f32[1,8,128]{2,1,0:T(8,128)S(1)} %pad_bitcast_fusion), channel_id=1, source_target_pairs={{0,1},{1,0},{2,3},{3,2},{4,5},{5,4},{6,7},{7,6},{8,9},{9,8},{10,11... | collective-permute-start | bytes 12296 | tf_op jit(solution)/shard_map/ppermute | solution.py:246
  21.5 0.8 reshape_squeeze.3
  22.3 0.7 pad_add_fusion.info
  22.9 0.0 collective-permute-done.4
  22.9 0.6 pad_maximum_fusion.3.col_pos
  23.5 0.0 collective-permute-done.3.far
  23.5 0.0 copy-start.1
  23.5 0.0 copy-done
  23.5 0.7 copy-done.1
  24.2 16.6 %pair_messages.1 = (f32[256,128]{1,0:T(8,128)}, bf16[4,64,128,256]{3,2,1,0:T(8,128)(2,1)}, bf16[4,128,128]{2,1,0:T(8,128)(2,1)}, f32[4,5,64,256]{3,2,1,0:T(8,128)}) custom-call(s32[11]{0:T(128)} %pad_add_fusion.info, bf16[8,144,128]{2,1,0:T(8,128)(2,1)} %copy-done, bf16[8,144,128]{2,1,0:T(8,128)(2,1)} %copy-done.1, f32[2,8,128]{2,1,0:T(8,128)} %pad_maximum_fusion.3.col_pos, ...), custom_call_target="tpu_custom_call" | custom-call | tf_op jit(solution)/shard_map/pair_messages/pallas_call | solution.py:311
  40.8 1.5 %collective-permute-start.5 = (f32[256,128]{1,0:T(8,128)}, f32[256,128]{1,0:T(8,128)S(1)}, u32[]{:S(2)}, u32[]{:S(2)}) collective-permute-start(f32[256,128]{1,0:T(8,128)} %get-tuple-element.9.msg_a), channel_id=1, source_target_pairs={{0,1},{1,0},{2,3},{3,2},{4,5},{5,4},{6,7},{7,6},{8,9},{9,8},{10,11... | collective-permute-start | bytes 393224 | tf_op jit(solution)/shard_map/ppermute | solution.py:246
  42.4 3.7 %collective-permute-done.5.msg_b = f32[256,128]{1,0:T(8,128)S(1)} collective-permute-done((f32[256,128]{1,0:T(8,128)}, f32[256,128]{1,0:T(8,128)S(1)}, u32[]{:S(2)}, u32[]{:S(2)}) %collective-permute-start.5) | collective-permute-done | bytes 131104 | tf_op jit(solution)/shard_map/ppermute | solution.py:246
  46.0 0.0 copy-start.2
  46.0 0.6 copy-done.2
  46.7 11.2 %pair_forces.1 = (bf16[128,128]{1,0:T(8,128)(2,1)}, f32[16,8,128]{2,1,0:T(8,128)}, f32[2,8,128]{2,1,0:T(8,128)}) custom-call(s32[11]{0:T(128)} %pad_add_fusion.info, f32[256,128]{1,0:T(8,128)} %get-tuple-element.9.msg_a, f32[256,128]{1,0:T(8,128)} %copy-done.2, bf16[128,128]{1,0:T(8,128)(2,1)} %features.1, bf16[128,128]{1,0:T(8,128)(2,1)} %w_o1.1, ...), custom_call_target="tpu_custom_call" | custom-call | tf_op jit(solution)/shard_map/pair_forces/pallas_call | solution.py:346
  57.9 0.8 slice.39
  58.6 6.2 %collective-permute-start.7 = (f32[8,8,128]{2,1,0:T(8,128)S(1)}, f32[8,8,128]{2,1,0:T(8,128)S(1)}, u32[]{:S(2)}, u32[]{:S(2)}) collective-permute-start(f32[8,8,128]{2,1,0:T(8,128)S(1)} %slice.39), channel_id=1, source_target_pairs={{0,2},{2,0},{4,6},{6,4},{8,10},{10,8},{12,14},{14,12},{16,18},{18,... | collective-permute-start | bytes 98312 | tf_op jit(solution)/shard_map/ppermute | solution.py:246
  64.8 0.9 collective-permute-done.7
  65.7 0.8 slice_add_fusion
  66.4 3.4 %collective-permute-start.8 = (f32[4,8,128]{2,1,0:T(8,128)S(1)}, f32[4,8,128]{2,1,0:T(8,128)S(1)}, u32[]{:S(2)}, u32[]{:S(2)}) collective-permute-start(f32[4,8,128]{2,1,0:T(8,128)S(1)} %slice.49), channel_id=1, source_target_pairs={{0,4},{2,6},{4,0},{6,2},{8,12},{10,14},{12,8},{14,10},{16,20},{18,... | collective-permute-start | bytes 49160 | tf_op jit(solution)/shard_map/ppermute | solution.py:246
  69.9 1.7 %collective-permute-done.8 = f32[4,8,128]{2,1,0:T(8,128)S(1)} collective-permute-done((f32[4,8,128]{2,1,0:T(8,128)S(1)}, f32[4,8,128]{2,1,0:T(8,128)S(1)}, u32[]{:S(2)}, u32[]{:S(2)}) %collective-permute-start.8) | collective-permute-done | bytes 16416 | tf_op jit(solution)/shard_map/ppermute | solution.py:246
  71.6 12.8 %collective-permute-start.9 = (f32[2,8,128]{2,1,0:T(8,128)S(1)}, f32[2,8,128]{2,1,0:T(8,128)S(1)}, u32[]{:S(2)}, u32[]{:S(2)}) collective-permute-start(f32[2,8,128]{2,1,0:T(8,128)S(1)} %slice.51), channel_id=1, source_target_pairs={{0,8},{2,10},{4,12},{6,14},{8,0},{10,2},{12,4},{14,6},{16,24},{18,... | collective-permute-start | bytes 24584 | tf_op jit(solution)/shard_map/ppermute | solution.py:246
  84.4 0.7 slice.37
  85.1 0.8 collective-permute-start.6
  86.0 0.1 collective-permute-done.9
  86.1 2.9 %collective-permute-start.10 = (f32[1,8,128]{2,1,0:T(8,128)S(1)}, f32[1,8,128]{2,1,0:T(8,128)S(1)}, u32[]{:S(2)}, u32[]{:S(2)}) collective-permute-start(f32[1,8,128]{2,1,0:T(8,128)S(1)} %slice.53), channel_id=1, source_target_pairs={{0,16},{2,18},{4,20},{6,22},{8,24},{10,26},{12,28},{14,30},{16,0},... | collective-permute-start | bytes 12296 | tf_op jit(solution)/shard_map/ppermute | solution.py:246
  89.0 0.0 collective-permute-done.6
  89.0 1.6 %collective-permute-done.10 = f32[1,8,128]{2,1,0:T(8,128)S(1)} collective-permute-done((f32[1,8,128]{2,1,0:T(8,128)S(1)}, f32[1,8,128]{2,1,0:T(8,128)S(1)}, u32[]{:S(2)}, u32[]{:S(2)}) %collective-permute-start.10) | collective-permute-done | bytes 4128 | tf_op jit(solution)/shard_map/ppermute | solution.py:246
  90.6 0.7 fusion
  91.3 0.6 slice_bitcast_fusion
  (9 shorter events, 0.1 us)
Async XLA Ops:
  2.2 6.4 %collective-permute-start = (bf16[1,144,128]{2,1,0:T(8,128)(2,1)S(1)}, bf16[1,144,128]{2,1,0:T(8,128)(2,1)S(1)}, u32[]{:S(2)}, u32[]{:S(2)}) collective-permute-start(bf16[1,144,128]{2,1,0:T(8,128)(2,1)S(1)} %bitcast.15), channel_id=1, source_target_pairs={{0,16},{2,18},{4,20},{6,22},{8,24},{10,26},{12,28},{14,30},{16,0},... | collective-permute-start | bytes 110600 | tf_op jit(solution)/shard_map/ppermute | solution.py:246
  8.7 4.4 %collective-permute-start.1 = (bf16[2,144,128]{2,1,0:T(8,128)(2,1)S(1)}, bf16[2,144,128]{2,1,0:T(8,128)(2,1)S(1)}, u32[]{:S(2)}, u32[]{:S(2)}) collective-permute-start(bf16[2,144,128]{2,1,0:T(8,128)(2,1)S(1)} %pad_maximum_fusion.2), channel_id=1, source_target_pairs={{0,8},{2,10},{4,12},{6,14},{8,0},{10,2},{12,4},{14,6},{16,24},{18,... | collective-permute-start | bytes 221192 | tf_op jit(solution)/shard_map/ppermute | solution.py:246
  13.1 5.2 %collective-permute-start.2 = (bf16[4,144,128]{2,1,0:T(8,128)(2,1)S(1)}, bf16[4,144,128]{2,1,0:T(8,128)(2,1)S(1)}, u32[]{:S(2)}, u32[]{:S(2)}) collective-permute-start(bf16[4,144,128]{2,1,0:T(8,128)(2,1)S(1)} %pad_maximum_fusion.1), channel_id=1, source_target_pairs={{0,4},{2,6},{4,0},{6,2},{8,12},{10,14},{12,8},{14,10},{16,20},{18,... | collective-permute-start | bytes 442376 | tf_op jit(solution)/shard_map/ppermute | solution.py:246
  18.3 5.2 %copy-start = (bf16[8,144,128]{2,1,0:T(8,128)(2,1)}, bf16[8,144,128]{2,1,0:T(8,128)(2,1)S(1)}, u32[]{:S(2)}) copy-start(bf16[8,144,128]{2,1,0:T(8,128)(2,1)S(1)} %pad_maximum_fusion.near) | copy-start | bytes 884740
  18.3 5.2 %collective-permute-start.3 = (bf16[8,144,128]{2,1,0:T(8,128)(2,1)S(1)}, bf16[8,144,128]{2,1,0:T(8,128)(2,1)S(1)}, u32[]{:S(2)}, u32[]{:S(2)}) collective-permute-start(bf16[8,144,128]{2,1,0:T(8,128)(2,1)S(1)} %pad_maximum_fusion.near), channel_id=1, source_target_pairs={{0,2},{2,0},{4,6},{6,4},{8,10},{10,8},{12,14},{14,12},{16,18},{18,... | collective-permute-start | bytes 884744 | tf_op jit(solution)/shard_map/ppermute | solution.py:246
  19.1 3.8 %collective-permute-start.4 = (f32[1,8,128]{2,1,0:T(8,128)S(1)}, f32[1,8,128]{2,1,0:T(8,128)S(1)}, u32[]{:S(2)}, u32[]{:S(2)}) collective-permute-start(f32[1,8,128]{2,1,0:T(8,128)S(1)} %pad_bitcast_fusion), channel_id=1, source_target_pairs={{0,1},{1,0},{2,3},{3,2},{4,5},{5,4},{6,7},{7,6},{8,9},{9,8},{10,11... | collective-permute-start | bytes 12296 | tf_op jit(solution)/shard_map/ppermute | solution.py:246
  23.5 0.7 copy-start.1
  40.8 5.2 %collective-permute-start.5 = (f32[256,128]{1,0:T(8,128)}, f32[256,128]{1,0:T(8,128)S(1)}, u32[]{:S(2)}, u32[]{:S(2)}) collective-permute-start(f32[256,128]{1,0:T(8,128)} %get-tuple-element.9.msg_a), channel_id=1, source_target_pairs={{0,1},{1,0},{2,3},{3,2},{4,5},{5,4},{6,7},{7,6},{8,9},{9,8},{10,11... | collective-permute-start | bytes 393224 | tf_op jit(solution)/shard_map/ppermute | solution.py:246
  46.0 0.6 copy-start.2
  58.6 7.1 %collective-permute-start.7 = (f32[8,8,128]{2,1,0:T(8,128)S(1)}, f32[8,8,128]{2,1,0:T(8,128)S(1)}, u32[]{:S(2)}, u32[]{:S(2)}) collective-permute-start(f32[8,8,128]{2,1,0:T(8,128)S(1)} %slice.39), channel_id=1, source_target_pairs={{0,2},{2,0},{4,6},{6,4},{8,10},{10,8},{12,14},{14,12},{16,18},{18,... | collective-permute-start | bytes 98312 | tf_op jit(solution)/shard_map/ppermute | solution.py:246
  66.4 5.2 %collective-permute-start.8 = (f32[4,8,128]{2,1,0:T(8,128)S(1)}, f32[4,8,128]{2,1,0:T(8,128)S(1)}, u32[]{:S(2)}, u32[]{:S(2)}) collective-permute-start(f32[4,8,128]{2,1,0:T(8,128)S(1)} %slice.49), channel_id=1, source_target_pairs={{0,4},{2,6},{4,0},{6,2},{8,12},{10,14},{12,8},{14,10},{16,20},{18,... | collective-permute-start | bytes 49160 | tf_op jit(solution)/shard_map/ppermute | solution.py:246
  71.6 14.5 %collective-permute-start.9 = (f32[2,8,128]{2,1,0:T(8,128)S(1)}, f32[2,8,128]{2,1,0:T(8,128)S(1)}, u32[]{:S(2)}, u32[]{:S(2)}) collective-permute-start(f32[2,8,128]{2,1,0:T(8,128)S(1)} %slice.51), channel_id=1, source_target_pairs={{0,8},{2,10},{4,12},{6,14},{8,0},{10,2},{12,4},{14,6},{16,24},{18,... | collective-permute-start | bytes 24584 | tf_op jit(solution)/shard_map/ppermute | solution.py:246
  85.1 3.9 %collective-permute-start.6 = (f32[1,8,128]{2,1,0:T(8,128)S(1)}, f32[1,8,128]{2,1,0:T(8,128)S(1)}, u32[]{:S(2)}, u32[]{:S(2)}) collective-permute-start(f32[1,8,128]{2,1,0:T(8,128)S(1)} %slice.37), channel_id=1, source_target_pairs={{0,1},{1,0},{2,3},{3,2},{4,5},{5,4},{6,7},{7,6},{8,9},{9,8},{10,11... | collective-permute-start | bytes 12296 | tf_op jit(solution)/shard_map/ppermute | solution.py:246
  86.1 4.5 %collective-permute-start.10 = (f32[1,8,128]{2,1,0:T(8,128)S(1)}, f32[1,8,128]{2,1,0:T(8,128)S(1)}, u32[]{:S(2)}, u32[]{:S(2)}) collective-permute-start(f32[1,8,128]{2,1,0:T(8,128)S(1)} %slice.53), channel_id=1, source_target_pairs={{0,16},{2,18},{4,20},{6,22},{8,24},{10,26},{12,28},{14,30},{16,0},... | collective-permute-start | bytes 12296 | tf_op jit(solution)/shard_map/ppermute | solution.py:246

commit v3 on v0

v3 whole, which is shorter than its diff:
```python
import math

import jax
import jax.numpy as jnp
from jax import lax
from jax.experimental import pallas as pl
from jax.experimental.pallas import tpu as pltpu
from jax.sharding import PartitionSpec as P

SOFTENING = 0.25
GAMMA_RBF = 10.0
CENTER_MAX = 10.0
CUTOFF = 12.0
LN2 = math.log(2.0)
SCALE = math.sqrt(GAMMA_RBF / LN2)
TANGENT = -GAMMA_RBF / SCALE
POS_ROWS = 16
CHUNK = 16
MIB = 1024 * 1024
F32 = jnp.float32
BF16 = jnp.bfloat16


def dot(a, b):
    return jnp.dot(a, b, preferred_element_type=F32)


def dot_t(a, b):
    return lax.dot_general(a, b, (((1,), (1,)), ((), ())), preferred_element_type=F32)


def split2(x):
    hi = x.astype(BF16)
    return hi, (x - hi.astype(F32)).astype(BF16)


def fold(x):
    half = x.shape[0] // 2
    return jnp.concatenate([x[:half], x[half:]], axis=1)


def unfold(x):
    half = x.shape[1] // 2
    return jnp.concatenate([x[:, :half], x[:, half:]], axis=0)


def block_diag(x):
    zero = jnp.zeros_like(x)
    return jnp.concatenate(
        [jnp.concatenate([x, zero], axis=1), jnp.concatenate([zero, x], axis=1)], axis=0
    )


def reverse_bits(value, count):
    bits = count.bit_length() - 1
    out = jnp.int32(0)
    for k in range(bits):
        out = out | (((value >> k) & 1) << (bits - 1 - k))
    return out


def out_type(shape, dtype):
    return pltpu.VMEM(shape, dtype)


def fetch(sources, targets, sems):
    copies = [
        pltpu.make_async_copy(src, dst, sems.at[k])
        for k, (src, dst) in enumerate(zip(sources, targets))
    ]
    for copy in copies:
        copy.start()
    for copy in copies:
        copy.wait()


def pack_kernel(features_hbm, positions_hbm, out, col_pos, features, positions, sems):
    fetch([features_hbm, positions_hbm], [features, positions], sems)
    n_feat = features.shape[0]
    col_pos[0] = jnp.concatenate([positions[...], jnp.zeros((5, positions.shape[1]), F32)], axis=0)
    out[0, :n_feat] = features[...]
    exact = positions[...]
    hi = exact.astype(BF16).astype(F32)
    mid = (exact - hi).astype(BF16).astype(F32)
    pad = jnp.zeros((POS_ROWS - 9, exact.shape[1]), F32)
    pieces = jnp.concatenate([hi, mid, exact - hi - mid, pad], axis=0)
    out[0, n_feat:] = pieces.astype(BF16)


def weight_kernel(
    w_in_hbm, w_f1_hbm, b_f1_hbm, w_f2_hbm, read_w_hbm, w_o2_hbm, w_o1_hbm, b_f2_hbm, b_o1_hbm, b_o2_hbm, masks_hbm,
    lhs, w2, w_in_t, direction, w_o2, w_o1, b_f2, b_o1, b_o2, masks,
    w_in, w_f1, b_f1, w_f2, read_w, sems,
):
    fetch(
        [
            w_in_hbm, w_f1_hbm, b_f1_hbm, w_f2_hbm, read_w_hbm, w_o2_hbm,
            w_o1_hbm, b_f2_hbm, b_o1_hbm, b_o2_hbm, masks_hbm,
        ],
        [w_in, w_f1, b_f1, w_f2, read_w, w_o2, w_o1, b_f2, b_o1, b_o2, masks],
        sems,
    )
    nbasis, hidden = w_f1.shape
    weights = w_f1[...].astype(F32)
    zero = jnp.zeros_like(weights)
    bias = b_f1[...] * 0.5
    b_hi = bias.astype(BF16).astype(F32)
    b_mid = (bias - b_hi).astype(BF16).astype(F32)
    b_lo = bias - b_hi - b_mid
    extra = jnp.concatenate([b_hi, b_mid, b_lo, jnp.zeros((13, hidden), F32)], axis=0)
    table = jnp.concatenate(
        [
            jnp.concatenate([0.5 * weights, zero], axis=1),
            jnp.concatenate([zero, weights], axis=1),
            jnp.concatenate([extra, jnp.zeros_like(extra)], axis=1),
            jnp.zeros((256 - 2 * nbasis - 16, 2 * hidden), F32),
        ],
        axis=0,
    )
    lhs[...] = table.T[:, : 2 * nbasis + 16].astype(BF16)
    wide = w_f2[...].astype(F32)
    w2[...] = jnp.concatenate([wide, wide], axis=1)
    w_in_t[...] = w_in[...].astype(F32).T.astype(BF16)
    readout = jnp.broadcast_to(read_w[...], (8, read_w.shape[1]))
    r_hi = readout.astype(BF16)
    r_mid, r_lo = split2(readout - r_hi.astype(F32))
    direction[...] = dot_t(r_hi, w_o2[...]) + (dot_t(r_mid, w_o2[...]) + dot_t(r_lo, w_o2[...]))


def pair_kernel(
    count, pairs, near, far, col_pos, masks, lhs, w2, w_in_t, b_f2,
    msg, tangents, proj_out, geom_out,
    diag, dist, coef_h, coef_x, rows, left,
):
    n_row = lax.axis_size("row")
    me_row = lax.axis_index("row")
    me_col = lax.axis_index("col")
    tile = masks.shape[2]
    hidden = w2.shape[0]
    nbasis = (lhs.shape[1] - 16) // 2
    msg[...] = jnp.zeros_like(msg)
    centers = lax.broadcasted_iota(jnp.int32, (nbasis, 2 * tile), 0).astype(F32) * (
        SCALE * CENTER_MAX / (nbasis - 1)
    )
    ones = jnp.ones((16, 2 * tile), BF16)

    @pl.loop(0, count[0, 0])
    def _(slot):
        row_tile, col_tile = pairs[0, 0, 0, slot], pairs[0, 0, 1, slot]
        place = reverse_bits(col_tile ^ me_row, n_row)
        half = n_row // 2
        index = place & (half - 1)
        block = jnp.where(place >= half, far[index], near[index])
        proj = dot(w_in_t[...], block[:tile]).astype(BF16)
        proj_out[slot] = proj
        proj_t = proj.astype(F32).T.astype(BF16)
        diag[...] = block_diag(proj_t)
        pieces = block[tile:].astype(F32)
        sender = pieces[0:3] + pieces[3:6] + pieces[6:9]
        receiver = col_pos[row_tile ^ me_col]
        square = jnp.zeros((tile, tile), F32)
        separation = []
        for k in range(3):
            up = jnp.broadcast_to(receiver[k : k + 1], (tile, tile)).T
            separation.append(up - sender[k : k + 1])
            square = square + separation[k] * separation[k]
        distance = jnp.sqrt(square + SOFTENING)
        angle = (math.pi / CUTOFF) * distance
        mask = masks[slot].astype(F32)
        cosine, sine = jnp.cos(angle), jnp.sin(angle)
        cut = 0.5 * (cosine + 1.0) * mask
        dist[...] = fold(distance * SCALE)
        coef_h[...] = fold(-LN2 * cut)
        coef_x[...] = fold(sine / (cosine + 1.0) * (LN2 * math.pi / CUTOFF / TANGENT))
        inverse = 1.0 / distance
        for k in range(3):
            geom_out[slot, k] = fold(separation[k] * inverse)
        geom_out[slot, 3] = fold((-0.5 * math.pi / CUTOFF) * sine * mask)
        geom_out[slot, 4] = fold(cut * TANGENT)
        c_hi, c_lo = split2(cut)
        bias_part = (dot(c_hi, proj_t) + dot(c_lo, proj_t)) * b_f2[...]

        @pl.loop(0, tile // 2 // CHUNK)
        def _(chunk):
            base = pl.multiple_of(chunk * CHUNK, CHUNK)
            here = pl.ds(base, CHUNK)
            d, h, x = dist[here, :], coef_h[here, :], coef_x[here, :]
            for u in range(CHUNK):
                offset = d[u : u + 1] - centers
                gauss = jnp.exp2(-(offset * offset))
                basis = jnp.concatenate(
                    [gauss.astype(BF16), (offset * gauss).astype(BF16), ones], axis=0
                )
                pre = dot(lhs[...], basis)
                bend = jnp.tanh(pre[:hidden])
                value = lax.log2(1.0 - bend)
                slope = (1.0 + bend) * pre[hidden:]
                left[pl.ds(u * hidden, hidden), :] = (h[u : u + 1] * value).astype(BF16)
                tangents[slot, base + u] = (x[u : u + 1] * value + slope).astype(BF16)
            mixed = dot(left[...], diag[...])
            sums = [
                jnp.sum(mixed[u * hidden : (u + 1) * hidden] * w2[...], axis=0, keepdims=True)
                for u in range(CHUNK)
            ]
            rows[here, :] = jnp.concatenate(sums, axis=0)

        here = pl.ds(pl.multiple_of(row_tile * tile, tile), tile)
        msg[here, :] = msg[here, :] + (bias_part + unfold(rows[...]))


def force_kernel(
    count, pairs, msg_a, msg_b, near, w_o1, b_o1, w_o2, b_o2, direction, w2, b_f2,
    proj, geom, tangents,
    features_out, keep, send, row_keep, row_send,
    grads, pre_act, diag, rows, left, force, row_force,
):
    n_row = lax.axis_size("row")
    n_col = lax.axis_size("col")
    me_row = lax.axis_index("row")
    me_col = lax.axis_index("col")
    n_feat, tile = features_out.shape
    hidden = w2.shape[0]
    force[...] = jnp.zeros_like(force)
    row_force[...] = jnp.zeros_like(row_force)
    messages = (msg_a[...] + msg_b[...]).astype(BF16)
    pre = dot(messages, w_o1[...]) + b_o1[...]
    pre_act[...] = pre
    s_hi, s_lo = split2(direction[0:1] / (1.0 + jnp.exp(-pre)))
    grads[...] = dot_t(s_hi, w_o1[...]) + dot_t(s_lo, w_o1[...])
    own = pre_act[pl.ds(pl.multiple_of(me_col * tile, tile), tile), :]
    active = jnp.maximum(own, 0.0) + jnp.log(1.0 + jnp.exp(-jnp.abs(own))) - LN2
    update = dot(active.astype(BF16), w_o2[...]) + b_o2[...]
    features_out[...] = (near[0, :n_feat].astype(F32) + update.T).astype(BF16)

    @pl.loop(0, count[0, 0])
    def _(slot):
        row_tile, col_tile = pairs[0, 0, 0, slot], pairs[0, 0, 1, slot]
        here = pl.ds(pl.multiple_of(row_tile * tile, tile), tile)
        grad_rows = grads[here, :]
        left_rows = fold(grad_rows)
        rows[...] = left_rows
        diag[...] = block_diag(proj[slot])

        @pl.loop(0, tile // 2 // CHUNK)
        def _(chunk):
            base = pl.multiple_of(chunk * CHUNK, CHUNK)
            here = pl.ds(base, CHUNK)
            g = rows[here, :]
            for u in range(CHUNK):
                left[pl.ds(u * hidden, hidden), :] = (w2[...] * g[u : u + 1]).astype(BF16)
            mixed = dot(left[...], diag[...])
            sums = [
                jnp.sum(
                    mixed[u * hidden : (u + 1) * hidden] * tangents[slot, base + u].astype(F32),
                    axis=0,
                    keepdims=True,
                )
                for u in range(CHUNK)
            ]
            rows[here, :] = jnp.concatenate(sums, axis=0)

        g_hi, g_lo = split2(grad_rows * b_f2[...])
        bias_part = dot(g_hi, proj[slot]) + dot(g_lo, proj[slot])
        dist_grad = unfold(geom[slot, 4] * rows[...]) + unfold(geom[slot, 3]) * bias_part
        to_rows, to_cols = [], []
        for k in range(3):
            push = unfold(geom[slot, k]) * dist_grad
            to_cols.append(jnp.sum(push, axis=0, keepdims=True))
            to_rows.append(-jnp.sum(push.T, axis=0, keepdims=True))
        zero = jnp.zeros((5, tile), F32)
        place = reverse_bits(col_tile ^ me_row, n_row)
        force[place] = force[place] + jnp.concatenate(to_cols + [zero], axis=0)
        place = reverse_bits(row_tile ^ me_col, n_col)
        row_force[place] = row_force[place] + jnp.concatenate(to_rows + [zero], axis=0)

    keep[...] = force[: n_row // 2]
    send[...] = force[n_row // 2 :]
    row_keep[...] = row_force[: n_col // 2]
    row_send[...] = row_force[n_col // 2 :]


def exchange(value, axis, size, step):
    return lax.ppermute(value, axis, [(i, i ^ step) for i in range(size)])


SMEM = pl.BlockSpec(memory_space=pltpu.SMEM)
VMEM = pl.BlockSpec(memory_space=pltpu.VMEM)
HBM = pl.BlockSpec(memory_space=pltpu.HBM)


def run(kernel, name, specs, out_shape, scratch, limit, *operands):
    return pl.pallas_call(
        kernel,
        in_specs=specs,
        out_specs=jax.tree.map(lambda _: VMEM, out_shape),
        out_shape=out_shape,
        scratch_shapes=scratch,
        compiler_params=pltpu.CompilerParams(vmem_limit_bytes=limit * MIB),
        name=name,
    )(*operands)


def local(
    features, positions, tile_pairs, pair_count, masks,
    w_in, w_f1, b_f1, w_f2, b_f2, w_o1, b_o1, w_o2, b_o2, read_w,
):
    n_feat, owned = features.shape
    tile = masks.shape[-1]
    tp = masks.shape[2]
    n_row = lax.axis_size("row")
    n_col = lax.axis_size("col")
    span = n_col * owned
    half = tile // 2
    nbasis, hidden = w_f1.shape

    near, col_pos = run(
        pack_kernel, "pack_tile", [HBM, HBM],
        [out_type((1, n_feat + POS_ROWS, owned), BF16), out_type((1, 8, owned), F32)],
        [
            pltpu.VMEM(features.shape, BF16),
            pltpu.VMEM(positions.shape, F32),
            pltpu.SemaphoreType.DMA((2,)),
        ],
        60,
        features, positions,
    )
    lhs, w2, w_in_t, direction, w_o2, w_o1, b_f2, b_o1, b_o2, masks = run(
        weight_kernel, "weight_tables", [HBM] * 11,
        [
            out_type((2 * hidden, 2 * nbasis + 16), BF16),
            out_type((hidden, 2 * n_feat), F32),
            out_type((n_feat, n_feat), BF16),
            out_type((8, n_feat), F32),
            out_type(w_o2.shape, BF16),
            out_type(w_o1.shape, BF16),
        ]
        + [out_type((1, n_feat), F32)] * 3
        + [out_type((tp, tile, tile), jnp.int32)],
        [
            pltpu.VMEM(w_in.shape, BF16),
            pltpu.VMEM(w_f1.shape, BF16),
            pltpu.VMEM((1, hidden), F32),
            pltpu.VMEM(w_f2.shape, BF16),
            pltpu.VMEM((1, n_feat), F32),
            pltpu.SemaphoreType.DMA((11,)),
        ],
        60,
        w_in, w_f1, b_f1[None], w_f2, read_w[None], w_o2, w_o1, b_f2[None], b_o1[None], b_o2[None],
        masks[0, 0],
    )
    step = n_row // 2
    while step > 1:
        near = jnp.concatenate([near, exchange(near, "row", n_row, step)], axis=0)
        step //= 2
    far = exchange(near, "row", n_row, 1)
    step = 1
    while step < n_col:
        col_pos = jnp.concatenate([col_pos, exchange(col_pos, "col", n_col, step)], axis=0)
        step *= 2
    count, pairs = pair_count, tile_pairs

    plane = pltpu.VMEM((half, 2 * tile), F32)
    partial, tangents, proj, geom = run(
        pair_kernel, "pair_messages", [SMEM, SMEM] + [VMEM] * 8,
        [
            out_type((span, n_feat), F32),
            out_type((tp, half, n_feat, 2 * tile), BF16),
            out_type((tp, n_feat, tile), BF16),
            out_type((tp, 5, half, 2 * tile), F32),
        ],
        [
            pltpu.VMEM((2 * tile, 2 * n_feat), BF16),
            plane, plane, plane, plane,
            pltpu.VMEM((CHUNK * hidden, 2 * tile), BF16),
        ],
        16,
        count, pairs, near, far, col_pos, masks, lhs, w2, w_in_t, b_f2,
    )

    step = 1
    while step < n_col // 2:
        partial = partial + exchange(partial, "col", n_col, step)
        step *= 2
    other = exchange(partial, "col", n_col, step)

    features_out, keep, send, row_keep, row_send = run(
        force_kernel, "pair_forces",
        [SMEM, SMEM] + [VMEM] * 13,
        [
            out_type((n_feat, owned), BF16),
            out_type((n_row // 2, 8, owned), F32),
            out_type((n_row // 2, 8, owned), F32),
            out_type((n_col // 2, 8, owned), F32),
            out_type((n_col // 2, 8, owned), F32),
        ],
        [
            pltpu.VMEM((span, n_feat), F32),
            pltpu.VMEM((span, n_feat), F32),
            pltpu.VMEM((2 * tile, 2 * n_feat), BF16),
            plane,
            pltpu.VMEM((CHUNK * hidden, 2 * n_feat), BF16),
            pltpu.VMEM((n_row, 8, owned), F32),
            pltpu.VMEM((n_col, 8, owned), F32),
        ],
        16,
        count, pairs, partial, other, near, w_o1, b_o1, w_o2, b_o2, direction, w2, b_f2,
        proj, geom, tangents,
    )

    def reduce_halves(keep, send, axis, size):
        step = 1
        while True:
            other = exchange(send, axis, size, step)
            half = keep.shape[0] // 2
            step *= 2
            if step == size:
                return (keep + other)[0]
            send = keep[half:] + other[half:]
            keep = keep[:half] + other[:half]

    forces = reduce_halves(keep, send, "row", n_row) + reduce_halves(
        row_keep, row_send, "col", n_col
    )
    return (features_out, forces[:3])


def solution(mesh):
    atoms = P(None, ("row", "col"))
    in_specs = (
        atoms,
        atoms,
        P("row", "col", None, None),
        P("row", "col"),
        P("row", "col", None, None, None),
    ) + (P(),) * 10
    return jax.shard_map(
        local, mesh=mesh, in_specs=in_specs, out_specs=(atoms, atoms), check_vma=False
    )
```

time: 356 us -> 74.3 us (0.21)
  matrix products: 132 us -> 0 us
  blocking collectives: 97.2 us -> 0 us
  waiting for transfers between devices: 64 us -> 18.6 us
  starting transfers between devices: 0.08 us -> 32.7 us
  Pallas kernels: 0 us -> 20 us
  loops' own time: 17.9 us -> 0 us
  local copies, waits for them, and re-layouts: 18 us -> 1.92 us
  between operations: 14.2 us -> 1.38 us
  other arithmetic: 12.7 us -> 0.05 us
    dot_general x21 -> x0, matrix products: 132 us -> none  [the longest x8 71.3 us: filter_forward(): jnp.einsum('hf,hrc->frc', w_f2, hidden, preferred_element_type=jnp.float32)]
    all_gather x2 -> x0, blocking collectives: 88.9 us -> none  [the longest x1 70.2 us: local(): lax.all_gather(positions, ('row', 'col'), axis=1, tiled=True)]
    unnamed x4 -> x0, waiting for transfers between devices: 64 us -> none
    ppermute x0 -> x11, starting transfers between devices: none -> 32.7 us  [exchange(): return lax.ppermute(value, axis, [(i, i ^ step) for i in range(size)])]
    pallas_call x0 -> x4, Pallas kernels: none -> 20 us  [run(): pl.pallas_call(kernel, in_specs=specs, out_specs=jax.tree.map(lambda _: V...]
    ppermute x0 -> x11, waiting for transfers between devices: none -> 18.6 us  [exchange(): return lax.ppermute(value, axis, [(i, i ^ step) for i in range(size)])]
    another operation x2 -> x0, loops' own time: 17.9 us -> none  [the longest x1 9.31 us: local(): lax.fori_loop(jnp.int32(0), pair_total, backward_slot, (jnp.zeros((3, row...]
    dynamic_slice x34 -> x0, local copies, waits for them, and re-layouts: 12.1 us -> none  [the longest x8 11.4 us: locate(): col_start = slot_pairs[1, slot_index] * tile]
  transfers between devices with their start and end apart: 2 -> 11, of which waited for: 2 -> 8; matrix products, arithmetic and copies ran while one was open for 1% -> 1% of each run, Pallas kernels for 0% -> 2%
where the time goes in v3:
time: 74.3 us; the launch traced here: 74.7 us
  starting transfers between devices  32.7 us (44%)
  Pallas kernels  20 us (27%)
  waiting for transfers between devices  18.6 us (25%)
  local copies, waits for them, and re-layouts  1.92 us (3%)
  between operations  1.38 us (2%)
    ppermute x11, starting transfers between devices, exchange(): return lax.ppermute(value, axis, [(i, i ^ step) for i in range(size)])  32.7 us
    pallas_call x4, Pallas kernels, run(): pl.pallas_call(kernel, in_specs=specs, out_specs=jax.tree.map(lambda _: V...  20 us
    ppermute x11, waiting for transfers between devices, exchange(): return lax.ppermute(value, axis, [(i, i ^ step) for i in range(size)])  18.6 us
  transfers between devices with their start and end apart: 11, of which 8 were waited for; matrix products, arithmetic and copies ran while one was open for 1% of the time, Pallas kernels for 2%

profile of v3, /device:TPU:0, one launch (start us, length us, event | category | flops | bytes accessed | tf_op | source)
XLA Modules:
  0.0 74.7 jit_solution(6189233150365586984)
XLA Ops:
  0.6 0.8 %pack_tile.1 = (bf16[1,144,128]{2,1,0:T(8,128)(2,1)S(1)}, f32[1,8,128]{2,1,0:T(8,128)S(1)}) custom-call(bf16[128,128]{1,0:T(8,128)(2,1)} %features_hbm.1, f32[3,128]{1,0:T(4,128)} %positions_hbm.1), custom_call_target="tpu_custom_call" | custom-call | tf_op jit(solution)/shard_map/pack_tile/pallas_call | solution.py:292
  1.4 4.1 %collective-permute-start = (bf16[1,144,128]{2,1,0:T(8,128)(2,1)S(1)}, bf16[1,144,128]{2,1,0:T(8,128)(2,1)S(1)}, u32[]{:S(2)}, u32[]{:S(2)}) collective-permute-start(bf16[1,144,128]{2,1,0:T(8,128)(2,1)S(1)} %get-tuple-element.23), channel_id=1, source_target_pairs={{0,16},{2,18},{4,20},{6,22},{8,24},{10,26},{12,28},{14,30},{16,0},... | collective-permute-start | bytes 110600 | tf_op jit(solution)/shard_map/ppermute | solution.py:283
  5.5 2.3 %collective-permute-done = bf16[1,144,128]{2,1,0:T(8,128)(2,1)S(1)} collective-permute-done((bf16[1,144,128]{2,1,0:T(8,128)(2,1)S(1)}, bf16[1,144,128]{2,1,0:T(8,128)(2,1)S(1)}, u32[]{:S(2)}, u32[]{:S(2)}) %collective-permute-start) | collective-permute-done | bytes 36896 | tf_op jit(solution)/shard_map/ppermute | solution.py:283
  7.9 1.6 %collective-permute-start.1 = (bf16[2,144,128]{2,1,0:T(8,128)(2,1)S(1)}, bf16[2,144,128]{2,1,0:T(8,128)(2,1)S(1)}, u32[]{:S(2)}, u32[]{:S(2)}) collective-permute-start(bf16[2,144,128]{2,1,0:T(8,128)(2,1)S(1)} %pad_maximum_fusion.1), channel_id=1, source_target_pairs={{0,8},{2,10},{4,12},{6,14},{8,0},{10,2},{12,4},{14,6},{16,24},{18,... | collective-permute-start | bytes 221192 | tf_op jit(solution)/shard_map/ppermute | solution.py:283
  9.5 2.8 %collective-permute-done.1 = bf16[2,144,128]{2,1,0:T(8,128)(2,1)S(1)} collective-permute-done((bf16[2,144,128]{2,1,0:T(8,128)(2,1)S(1)}, bf16[2,144,128]{2,1,0:T(8,128)(2,1)S(1)}, u32[]{:S(2)}, u32[]{:S(2)}) %collective-permute-start.1) | collective-permute-done | bytes 73760 | tf_op jit(solution)/shard_map/ppermute | solution.py:283
  12.3 1.8 %collective-permute-start.2 = (bf16[4,144,128]{2,1,0:T(8,128)(2,1)S(1)}, bf16[4,144,128]{2,1,0:T(8,128)(2,1)S(1)}, u32[]{:S(2)}, u32[]{:S(2)}) collective-permute-start(bf16[4,144,128]{2,1,0:T(8,128)(2,1)S(1)} %pad_maximum_fusion), channel_id=1, source_target_pairs={{0,4},{2,6},{4,0},{6,2},{8,12},{10,14},{12,8},{14,10},{16,20},{18,... | collective-permute-start | bytes 442376 | tf_op jit(solution)/shard_map/ppermute | solution.py:283
  14.1 3.4 %collective-permute-done.2 = bf16[4,144,128]{2,1,0:T(8,128)(2,1)S(1)} collective-permute-done((bf16[4,144,128]{2,1,0:T(8,128)(2,1)S(1)}, bf16[4,144,128]{2,1,0:T(8,128)(2,1)S(1)}, u32[]{:S(2)}, u32[]{:S(2)}) %collective-permute-start.2) | collective-permute-done | bytes 147488 | tf_op jit(solution)/shard_map/ppermute | solution.py:283
  17.5 0.1 collective-permute-start.3
  17.6 1.8 %collective-permute-start.4 = (f32[1,8,128]{2,1,0:T(8,128)S(1)}, f32[1,8,128]{2,1,0:T(8,128)S(1)}, u32[]{:S(2)}, u32[]{:S(2)}) collective-permute-start(f32[1,8,128]{2,1,0:T(8,128)S(1)} %get-tuple-element.24), channel_id=1, source_target_pairs={{0,1},{1,0},{2,3},{3,2},{4,5},{5,4},{6,7},{7,6},{8,9},{9,8},{10,11... | collective-permute-start | bytes 12296 | tf_op jit(solution)/shard_map/ppermute | solution.py:283
  20.0 1.4 %weight_tables.1 = (bf16[256,144]{1,0:T(8,128)(2,1)S(1)}, f32[128,256]{1,0:T(8,128)S(1)}, bf16[128,128]{1,0:T(8,128)(2,1)S(1)}, f32[8,128]{1,0:T(8,128)S(1)}, bf...) custom-call(bf16[128,128]{1,0:T(8,128)(2,1)} %w_in_hbm.1, ...), custom_call_target="tpu_custom_call" | custom-call | tf_op jit(solution)/shard_map/weight_tables/pallas_call | solution.py:292
  21.4 0.0 collective-permute-done.4
  21.5 0.0 collective-permute-done.3.far
  21.5 0.0 copy-start
  21.5 0.7 copy-done
  22.2 12.4 %pair_messages.1 = (f32[256,128]{1,0:T(8,128)S(1)}, bf16[4,64,128,256]{3,2,1,0:T(8,128)(2,1)S(1)}, bf16[4,128,128]{2,1,0:T(8,128)(2,1)S(1)}, f32[4,5,64,256]{3,2,1,0:T(8,128)S(1)}) custom-call(s32[1,1]{1,0:T(1,128)S(6)} %copy.21.count, s32[1,1,2,4]{3,2,1,0:T(2,128)S(1)} %copy-done, bf16[8,144,128]{2,1,0:T(8,128)(2,1)S(1)} %constant_dynamic-update-slice_fusion.near, ...), custom_call_target="tpu_custom_call" | custom-call | tf_op jit(solution)/shard_map/pair_messages/pallas_call | solution.py:292
  34.6 13.5 %collective-permute-start.5 = (f32[256,128]{1,0:T(8,128)S(1)}, f32[256,128]{1,0:T(8,128)S(1)}, u32[]{:S(2)}, u32[]{:S(2)}) collective-permute-start(f32[256,128]{1,0:T(8,128)S(1)} %get-tuple-element.30.msg_a), channel_id=1, source_target_pairs={{0,1},{1,0},{2,3},{3,2},{4,5},{5,4},{6,7},{7,6},{8,9},{9,8},{10,11... | collective-permute-start | bytes 393224 | tf_op jit(solution)/shard_map/ppermute | solution.py:283
  48.1 2.9 %collective-permute-done.5.msg_b = f32[256,128]{1,0:T(8,128)S(1)} collective-permute-done((f32[256,128]{1,0:T(8,128)S(1)}, f32[256,128]{1,0:T(8,128)S(1)}, u32[]{:S(2)}, u32[]{:S(2)}) %collective-permute-start.5) | collective-permute-done | bytes 131104 | tf_op jit(solution)/shard_map/ppermute | solution.py:283
  51.0 5.4 %pair_forces.1 = (bf16[128,128]{1,0:T(8,128)(2,1)S(1)}, f32[8,8,128]{2,1,0:T(8,128)S(1)}, f32[8,8,128]{2,1,0:T(8,128)S(1)}, f32[1,8,128]{2,1,0:T(8,128)S(1)}, f32[1,8,128]{2,1,0:T(8,128)S(1)}) custom-call(s32[1,1]{1,0:T(1,128)S(6)} %copy.21.count, s32[1,1,2,4]{3,2,1,0:T(2,128)S(1)} %copy-done, f32[256,128]{1,0:T(8,128)S(1)} %get-tuple-element.30.msg_a, ...), custom_call_target="tpu_custom_call" | custom-call | tf_op jit(solution)/shard_map/pair_forces/pallas_call | solution.py:292
  56.4 0.1 collective-permute-start.6
  56.5 1.2 %collective-permute-done.6 = f32[8,8,128]{2,1,0:T(8,128)S(1)} collective-permute-done((f32[8,8,128]{2,1,0:T(8,128)S(1)}, f32[8,8,128]{2,1,0:T(8,128)S(1)}, u32[]{:S(2)}, u32[]{:S(2)}) %collective-permute-start.6) | collective-permute-done | bytes 32800 | tf_op jit(solution)/shard_map/ppermute | solution.py:283
  57.7 6.5 %collective-permute-start.7 = (f32[4,8,128]{2,1,0:T(8,128)S(1)}, f32[4,8,128]{2,1,0:T(8,128)S(1)}, u32[]{:S(2)}, u32[]{:S(2)}) collective-permute-start(f32[4,8,128]{2,1,0:T(8,128)S(1)} %get-tuple-element.45), channel_id=1, source_target_pairs={{0,4},{2,6},{4,0},{6,2},{8,12},{10,14},{12,8},{14,10},{16,20},{18,... | collective-permute-start | bytes 49160 | tf_op jit(solution)/shard_map/ppermute | solution.py:283
  64.2 1.7 %collective-permute-done.7 = f32[4,8,128]{2,1,0:T(8,128)S(1)} collective-permute-done((f32[4,8,128]{2,1,0:T(8,128)S(1)}, f32[4,8,128]{2,1,0:T(8,128)S(1)}, u32[]{:S(2)}, u32[]{:S(2)}) %collective-permute-start.7) | collective-permute-done | bytes 16416 | tf_op jit(solution)/shard_map/ppermute | solution.py:283
  65.9 0.0 collective-permute-start.8
  65.9 2.1 %collective-permute-start.10 = (f32[1,8,128]{2,1,0:T(8,128)S(1)}, f32[1,8,128]{2,1,0:T(8,128)S(1)}, u32[]{:S(2)}, u32[]{:S(2)}) collective-permute-start(f32[1,8,128]{2,1,0:T(8,128)S(1)} %get-tuple-element.43), channel_id=1, source_target_pairs={{0,1},{1,0},{2,3},{3,2},{4,5},{5,4},{6,7},{7,6},{8,9},{9,8},{10,11... | collective-permute-start | bytes 12296 | tf_op jit(solution)/shard_map/ppermute | solution.py:283
  68.0 1.6 %collective-permute-done.8 = f32[2,8,128]{2,1,0:T(8,128)S(1)} collective-permute-done((f32[2,8,128]{2,1,0:T(8,128)S(1)}, f32[2,8,128]{2,1,0:T(8,128)S(1)}, u32[]{:S(2)}, u32[]{:S(2)}) %collective-permute-start.8) | collective-permute-done | bytes 8224 | tf_op jit(solution)/shard_map/ppermute | solution.py:283
  69.6 1.3 %collective-permute-start.9 = (f32[1,8,128]{2,1,0:T(8,128)S(1)}, f32[1,8,128]{2,1,0:T(8,128)S(1)}, u32[]{:S(2)}, u32[]{:S(2)}) collective-permute-start(f32[1,8,128]{2,1,0:T(8,128)S(1)} %slice_add_fusion.4), channel_id=1, source_target_pairs={{0,16},{2,18},{4,20},{6,22},{8,24},{10,26},{12,28},{14,30},{16,0},... | collective-permute-start | bytes 12296 | tf_op jit(solution)/shard_map/ppermute | solution.py:283
  70.9 0.6 copy.20
  71.5 0.0 collective-permute-done.10
  71.5 2.6 %collective-permute-done.9 = f32[1,8,128]{2,1,0:T(8,128)S(1)} collective-permute-done((f32[1,8,128]{2,1,0:T(8,128)S(1)}, f32[1,8,128]{2,1,0:T(8,128)S(1)}, u32[]{:S(2)}, u32[]{:S(2)}) %collective-permute-start.9) | collective-permute-done | bytes 4128 | tf_op jit(solution)/shard_map/ppermute | solution.py:283
  74.1 0.6 slice_bitcast_fusion
  (11 shorter events, 0.1 us)
Async XLA Ops:
  1.4 6.4 %collective-permute-start = (bf16[1,144,128]{2,1,0:T(8,128)(2,1)S(1)}, bf16[1,144,128]{2,1,0:T(8,128)(2,1)S(1)}, u32[]{:S(2)}, u32[]{:S(2)}) collective-permute-start(bf16[1,144,128]{2,1,0:T(8,128)(2,1)S(1)} %get-tuple-element.23), channel_id=1, source_target_pairs={{0,16},{2,18},{4,20},{6,22},{8,24},{10,26},{12,28},{14,30},{16,0},... | collective-permute-start | bytes 110600 | tf_op jit(solution)/shard_map/ppermute | solution.py:283
  7.9 4.4 %collective-permute-start.1 = (bf16[2,144,128]{2,1,0:T(8,128)(2,1)S(1)}, bf16[2,144,128]{2,1,0:T(8,128)(2,1)S(1)}, u32[]{:S(2)}, u32[]{:S(2)}) collective-permute-start(bf16[2,144,128]{2,1,0:T(8,128)(2,1)S(1)} %pad_maximum_fusion.1), channel_id=1, source_target_pairs={{0,8},{2,10},{4,12},{6,14},{8,0},{10,2},{12,4},{14,6},{16,24},{18,... | collective-permute-start | bytes 221192 | tf_op jit(solution)/shard_map/ppermute | solution.py:283
  12.3 5.2 %collective-permute-start.2 = (bf16[4,144,128]{2,1,0:T(8,128)(2,1)S(1)}, bf16[4,144,128]{2,1,0:T(8,128)(2,1)S(1)}, u32[]{:S(2)}, u32[]{:S(2)}) collective-permute-start(bf16[4,144,128]{2,1,0:T(8,128)(2,1)S(1)} %pad_maximum_fusion), channel_id=1, source_target_pairs={{0,4},{2,6},{4,0},{6,2},{8,12},{10,14},{12,8},{14,10},{16,20},{18,... | collective-permute-start | bytes 442376 | tf_op jit(solution)/shard_map/ppermute | solution.py:283
  17.5 3.9 %collective-permute-start.3 = (bf16[8,144,128]{2,1,0:T(8,128)(2,1)S(1)}, bf16[8,144,128]{2,1,0:T(8,128)(2,1)S(1)}, u32[]{:S(2)}, u32[]{:S(2)}) collective-permute-start(bf16[8,144,128]{2,1,0:T(8,128)(2,1)S(1)} %constant_dynamic-update-slice_fusion.near), channel_id=1, source_target_pairs={{0,2},{2,0},{4,6},{6,4},{8,10},{10,8},{12,14},{14,12},{16,18},{18,... | collective-permute-start | bytes 884744 | tf_op jit(solution)/shard_map/ppermute | solution.py:283
  17.6 3.8 %collective-permute-start.4 = (f32[1,8,128]{2,1,0:T(8,128)S(1)}, f32[1,8,128]{2,1,0:T(8,128)S(1)}, u32[]{:S(2)}, u32[]{:S(2)}) collective-permute-start(f32[1,8,128]{2,1,0:T(8,128)S(1)} %get-tuple-element.24), channel_id=1, source_target_pairs={{0,1},{1,0},{2,3},{3,2},{4,5},{5,4},{6,7},{7,6},{8,9},{9,8},{10,11... | collective-permute-start | bytes 12296 | tf_op jit(solution)/shard_map/ppermute | solution.py:283
  21.5 0.7 copy-start
  34.6 16.4 %collective-permute-start.5 = (f32[256,128]{1,0:T(8,128)S(1)}, f32[256,128]{1,0:T(8,128)S(1)}, u32[]{:S(2)}, u32[]{:S(2)}) collective-permute-start(f32[256,128]{1,0:T(8,128)S(1)} %get-tuple-element.30.msg_a), channel_id=1, source_target_pairs={{0,1},{1,0},{2,3},{3,2},{4,5},{5,4},{6,7},{7,6},{8,9},{9,8},{10,11... | collective-permute-start | bytes 393224 | tf_op jit(solution)/shard_map/ppermute | solution.py:283
  56.4 1.3 %collective-permute-start.6 = (f32[8,8,128]{2,1,0:T(8,128)S(1)}, f32[8,8,128]{2,1,0:T(8,128)S(1)}, u32[]{:S(2)}, u32[]{:S(2)}) collective-permute-start(f32[8,8,128]{2,1,0:T(8,128)S(1)} %get-tuple-element.41), channel_id=1, source_target_pairs={{0,2},{2,0},{4,6},{6,4},{8,10},{10,8},{12,14},{14,12},{16,18},{18,... | collective-permute-start | bytes 98312 | tf_op jit(solution)/shard_map/ppermute | solution.py:283
  57.7 8.2 %collective-permute-start.7 = (f32[4,8,128]{2,1,0:T(8,128)S(1)}, f32[4,8,128]{2,1,0:T(8,128)S(1)}, u32[]{:S(2)}, u32[]{:S(2)}) collective-permute-start(f32[4,8,128]{2,1,0:T(8,128)S(1)} %get-tuple-element.45), channel_id=1, source_target_pairs={{0,4},{2,6},{4,0},{6,2},{8,12},{10,14},{12,8},{14,10},{16,20},{18,... | collective-permute-start | bytes 49160 | tf_op jit(solution)/shard_map/ppermute | solution.py:283
  65.9 3.7 %collective-permute-start.8 = (f32[2,8,128]{2,1,0:T(8,128)S(1)}, f32[2,8,128]{2,1,0:T(8,128)S(1)}, u32[]{:S(2)}, u32[]{:S(2)}) collective-permute-start(f32[2,8,128]{2,1,0:T(8,128)S(1)} %get-tuple-element.47), channel_id=1, source_target_pairs={{0,8},{2,10},{4,12},{6,14},{8,0},{10,2},{12,4},{14,6},{16,24},{18,... | collective-permute-start | bytes 24584 | tf_op jit(solution)/shard_map/ppermute | solution.py:283
  65.9 5.6 %collective-permute-start.10 = (f32[1,8,128]{2,1,0:T(8,128)S(1)}, f32[1,8,128]{2,1,0:T(8,128)S(1)}, u32[]{:S(2)}, u32[]{:S(2)}) collective-permute-start(f32[1,8,128]{2,1,0:T(8,128)S(1)} %get-tuple-element.43), channel_id=1, source_target_pairs={{0,1},{1,0},{2,3},{3,2},{4,5},{5,4},{6,7},{7,6},{8,9},{9,8},{10,11... | collective-permute-start | bytes 12296 | tf_op jit(solution)/shard_map/ppermute | solution.py:283
  69.6 4.5 %collective-permute-start.9 = (f32[1,8,128]{2,1,0:T(8,128)S(1)}, f32[1,8,128]{2,1,0:T(8,128)S(1)}, u32[]{:S(2)}, u32[]{:S(2)}) collective-permute-start(f32[1,8,128]{2,1,0:T(8,128)S(1)} %slice_add_fusion.4), channel_id=1, source_target_pairs={{0,16},{2,18},{4,20},{6,22},{8,24},{10,26},{12,28},{14,30},{16,0},... | collective-permute-start | bytes 12296 | tf_op jit(solution)/shard_map/ppermute | solution.py:283

commit v4 on v3

--- a/solution.py
+++ b/solution.py
@@ -63,6 +63,21 @@
     return pltpu.VMEM(shape, dtype)
 
 
+def spread(row, count):
+    rows = jnp.broadcast_to(row, (16, row.shape[1])).astype(BF16)
+    return jnp.concatenate([rows] * (count // 16), axis=0)
+
+
+def sin_cos(angle):
+    turn = angle - 0.5 * math.pi
+    square = turn * turn
+    odd, even = 0.0, 0.0
+    for k in range(6, -1, -1):
+        odd = odd * square + (-1.0) ** k / math.factorial(2 * k + 1)
+        even = even * square + (-1.0) ** k / math.factorial(2 * k)
+    return even, -(odd * turn)
+
+
 def fetch(sources, targets, sems):
     copies = [
         pltpu.make_async_copy(src, dst, sems.at[k])
@@ -87,17 +102,23 @@
     out[0, n_feat:] = pieces.astype(BF16)
 
 
+def stack_kernel(held, got, *rest):
+    out = rest[-1]
+    out[: held.shape[0]] = held[...]
+    out[held.shape[0] :] = got[...]
+
+
 def weight_kernel(
-    w_in_hbm, w_f1_hbm, b_f1_hbm, w_f2_hbm, read_w_hbm, w_o2_hbm, w_o1_hbm, b_f2_hbm, b_o1_hbm, b_o2_hbm, masks_hbm,
-    lhs, w2, w_in_t, direction, w_o2, w_o1, b_f2, b_o1, b_o2, masks,
+    w_in_hbm, w_f1_hbm, b_f1_hbm, w_f2_hbm, read_w_hbm, w_o2_hbm, w_o1_hbm, b_f2_hbm, b_o1_hbm, b_o2_hbm, masks_hbm, pairs_hbm,
+    lhs, w2, w2_16, w_in_t, direction, w_o2, w_o1, b_f2, b_o1, b_o2, masks, pairs,
     w_in, w_f1, b_f1, w_f2, read_w, sems,
 ):
     fetch(
         [
             w_in_hbm, w_f1_hbm, b_f1_hbm, w_f2_hbm, read_w_hbm, w_o2_hbm,
-            w_o1_hbm, b_f2_hbm, b_o1_hbm, b_o2_hbm, masks_hbm,
-        ],
-        [w_in, w_f1, b_f1, w_f2, read_w, w_o2, w_o1, b_f2, b_o1, b_o2, masks],
+            w_o1_hbm, b_f2_hbm, b_o1_hbm, b_o2_hbm, masks_hbm, pairs_hbm,
+        ],
+        [w_in, w_f1, b_f1, w_f2, read_w, w_o2, w_o1, b_f2, b_o1, b_o2, masks, pairs],
         sems,
     )
     nbasis, hidden = w_f1.shape
@@ -120,6 +141,7 @@
     lhs[...] = table.T[:, : 2 * nbasis + 16].astype(BF16)
     wide = w_f2[...].astype(F32)
     w2[...] = jnp.concatenate([wide, wide], axis=1)
+    w2_16[...] = w2[...].astype(BF16)
     w_in_t[...] = w_in[...].astype(F32).T.astype(BF16)
     readout = jnp.broadcast_to(read_w[...], (8, read_w.shape[1]))
     r_hi = readout.astype(BF16)
@@ -129,7 +151,7 @@
 
 def pair_kernel(
     count, pairs, near, far, col_pos, masks, lhs, w2, w_in_t, b_f2,
-    msg, tangents, proj_out, geom_out,
+    msg, msg16, tangents, proj_out, geom_out,
     diag, dist, coef_h, coef_x, rows, left,
 ):
     n_row = lax.axis_size("row")
@@ -167,7 +189,7 @@
         distance = jnp.sqrt(square + SOFTENING)
         angle = (math.pi / CUTOFF) * distance
         mask = masks[slot].astype(F32)
-        cosine, sine = jnp.cos(angle), jnp.sin(angle)
+        sine, cosine = sin_cos(angle)
         cut = 0.5 * (cosine + 1.0) * mask
         dist[...] = fold(distance * SCALE)
         coef_h[...] = fold(-LN2 * cut)
@@ -195,8 +217,9 @@
                 bend = jnp.tanh(pre[:hidden])
                 value = lax.log2(1.0 - bend)
                 slope = (1.0 + bend) * pre[hidden:]
-                left[pl.ds(u * hidden, hidden), :] = (h[u : u + 1] * value).astype(BF16)
-                tangents[slot, base + u] = (x[u : u + 1] * value + slope).astype(BF16)
+                value = value.astype(BF16)
+                left[pl.ds(u * hidden, hidden), :] = spread(h[u : u + 1], hidden) * value
+                tangents[slot, base + u] = spread(x[u : u + 1], hidden) * value + slope.astype(BF16)
             mixed = dot(left[...], diag[...])
             sums = [
                 jnp.sum(mixed[u * hidden : (u + 1) * hidden] * w2[...], axis=0, keepdims=True)
@@ -207,22 +230,24 @@
         here = pl.ds(pl.multiple_of(row_tile * tile, tile), tile)
         msg[here, :] = msg[here, :] + (bias_part + unfold(rows[...]))
 
+    msg16[...] = msg[...].astype(BF16)
+
 
 def force_kernel(
-    count, pairs, msg_a, msg_b, near, w_o1, b_o1, w_o2, b_o2, direction, w2, b_f2,
+    count, pairs, msg_a, msg_b, near, w_o1, b_o1, w_o2, b_o2, direction, w2_16, b_f2,
     proj, geom, tangents,
-    features_out, keep, send, row_keep, row_send,
-    grads, pre_act, diag, rows, left, force, row_force,
+    features_hbm, keep, send, row_keep, row_send,
+    features_out, grads, pre_act, diag, rows, left, force, row_force, sems,
 ):
     n_row = lax.axis_size("row")
     n_col = lax.axis_size("col")
     me_row = lax.axis_index("row")
     me_col = lax.axis_index("col")
     n_feat, tile = features_out.shape
-    hidden = w2.shape[0]
+    hidden = w2_16.shape[0]
     force[...] = jnp.zeros_like(force)
     row_force[...] = jnp.zeros_like(row_force)
-    messages = (msg_a[...] + msg_b[...]).astype(BF16)
+    messages = (msg_a[...] + msg_b[...].astype(F32)).astype(BF16)
     pre = dot(messages, w_o1[...]) + b_o1[...]
     pre_act[...] = pre
     s_hi, s_lo = split2(direction[0:1] / (1.0 + jnp.exp(-pre)))
@@ -231,6 +256,8 @@
     active = jnp.maximum(own, 0.0) + jnp.log(1.0 + jnp.exp(-jnp.abs(own))) - LN2
     update = dot(active.astype(BF16), w_o2[...]) + b_o2[...]
     features_out[...] = (near[0, :n_feat].astype(F32) + update.T).astype(BF16)
+    store = pltpu.make_async_copy(features_out, features_hbm, sems.at[0])
+    store.start()
 
     @pl.loop(0, count[0, 0])
     def _(slot):
@@ -247,7 +274,7 @@
             here = pl.ds(base, CHUNK)
             g = rows[here, :]
             for u in range(CHUNK):
-                left[pl.ds(u * hidden, hidden), :] = (w2[...] * g[u : u + 1]).astype(BF16)
+                left[pl.ds(u * hidden, hidden), :] = w2_16[...] * spread(g[u : u + 1], hidden)
             mixed = dot(left[...], diag[...])
             sums = [
                 jnp.sum(
@@ -277,12 +304,14 @@
     send[...] = force[n_row // 2 :]
     row_keep[...] = row_force[: n_col // 2]
     row_send[...] = row_force[n_col // 2 :]
+    store.wait()
 
 
 def exchange(value, axis, size, step):
     return lax.ppermute(value, axis, [(i, i ^ step) for i in range(size)])
 
 
+ANY = pl.BlockSpec(memory_space=pl.ANY)
 SMEM = pl.BlockSpec(memory_space=pltpu.SMEM)
 VMEM = pl.BlockSpec(memory_space=pltpu.VMEM)
 HBM = pl.BlockSpec(memory_space=pltpu.HBM)
@@ -292,7 +321,7 @@
     return pl.pallas_call(
         kernel,
         in_specs=specs,
-        out_specs=jax.tree.map(lambda _: VMEM, out_shape),
+        out_specs=[pl.BlockSpec(memory_space=x.memory_space) for x in out_shape],
         out_shape=out_shape,
         scratch_shapes=scratch,
         compiler_params=pltpu.CompilerParams(vmem_limit_bytes=limit * MIB),
@@ -324,46 +353,59 @@
         60,
         features, positions,
     )
-    lhs, w2, w_in_t, direction, w_o2, w_o1, b_f2, b_o1, b_o2, masks = run(
-        weight_kernel, "weight_tables", [HBM] * 11,
+    lhs, w2, w2_16, w_in_t, direction, w_o2, w_o1, b_f2, b_o1, b_o2, masks, pairs = run(
+        weight_kernel, "weight_tables", [HBM] * 12,
         [
             out_type((2 * hidden, 2 * nbasis + 16), BF16),
             out_type((hidden, 2 * n_feat), F32),
+            out_type((hidden, 2 * n_feat), BF16),
             out_type((n_feat, n_feat), BF16),
             out_type((8, n_feat), F32),
             out_type(w_o2.shape, BF16),
             out_type(w_o1.shape, BF16),
         ]
         + [out_type((1, n_feat), F32)] * 3
-        + [out_type((tp, tile, tile), jnp.int32)],
+        + [out_type((tp, tile, tile), jnp.int32), pltpu.SMEM(tile_pairs.shape, jnp.int32)],
         [
             pltpu.VMEM(w_in.shape, BF16),
             pltpu.VMEM(w_f1.shape, BF16),
             pltpu.VMEM((1, hidden), F32),
             pltpu.VMEM(w_f2.shape, BF16),
             pltpu.VMEM((1, n_feat), F32),
-            pltpu.SemaphoreType.DMA((11,)),
+            pltpu.SemaphoreType.DMA((12,)),
         ],
         60,
         w_in, w_f1, b_f1[None], w_f2, read_w[None], w_o2, w_o1, b_f2[None], b_o1[None], b_o2[None],
-        masks[0, 0],
-    )
-    step = n_row // 2
-    while step > 1:
-        near = jnp.concatenate([near, exchange(near, "row", n_row, step)], axis=0)
-        step //= 2
-    far = exchange(near, "row", n_row, 1)
+        masks[0, 0], tile_pairs,
+    )
+    col_pos = col_pos
     step = 1
     while step < n_col:
         col_pos = jnp.concatenate([col_pos, exchange(col_pos, "col", n_col, step)], axis=0)
         step *= 2
-    count, pairs = pair_count, tile_pairs
+
+    def stack(held, got, *after):
+        return run(
+            stack_kernel, "stack_tiles", [VMEM, VMEM] + [ANY] * len(after),
+            [out_type((2 * held.shape[0],) + held.shape[1:], BF16)], [], 4,
+            held, got, *after,
+        )[0]
+
+    ready = [[w2], [col_pos]]
+    own = near
+    step = n_row // 2
+    while step > 1:
+        near = stack(near, exchange(near, "row", n_row, step), *(ready.pop(0) if ready else []))
+        step //= 2
+    far = exchange(near, "row", n_row, 1)
+    count = pair_count
 
     plane = pltpu.VMEM((half, 2 * tile), F32)
-    partial, tangents, proj, geom = run(
+    partial, partial16, tangents, proj, geom = run(
         pair_kernel, "pair_messages", [SMEM, SMEM] + [VMEM] * 8,
         [
             out_type((span, n_feat), F32),
+            out_type((span, n_feat), BF16),
             out_type((tp, half, n_feat, 2 * tile), BF16),
             out_type((tp, n_feat, tile), BF16),
             out_type((tp, 5, half, 2 * tile), F32),
@@ -379,21 +421,23 @@
 
     step = 1
     while step < n_col // 2:
-        partial = partial + exchange(partial, "col", n_col, step)
+        partial = partial + exchange(partial16, "col", n_col, step).astype(F32)
+        partial16 = partial.astype(BF16)
         step *= 2
-    other = exchange(partial, "col", n_col, step)
+    other = exchange(partial16, "col", n_col, step)
 
     features_out, keep, send, row_keep, row_send = run(
         force_kernel, "pair_forces",
         [SMEM, SMEM] + [VMEM] * 13,
         [
-            out_type((n_feat, owned), BF16),
+            pltpu.HBM((n_feat, owned), BF16),
             out_type((n_row // 2, 8, owned), F32),
             out_type((n_row // 2, 8, owned), F32),
             out_type((n_col // 2, 8, owned), F32),
             out_type((n_col // 2, 8, owned), F32),
         ],
         [
+            pltpu.VMEM((n_feat, owned), BF16),
             pltpu.VMEM((span, n_feat), F32),
             pltpu.VMEM((span, n_feat), F32),
             pltpu.VMEM((2 * tile, 2 * n_feat), BF16),
@@ -401,9 +445,10 @@
             pltpu.VMEM((CHUNK * hidden, 2 * n_feat), BF16),
             pltpu.VMEM((n_row, 8, owned), F32),
             pltpu.VMEM((n_col, 8, owned), F32),
+            pltpu.SemaphoreType.DMA((1,)),
         ],
         16,
-        count, pairs, partial, other, near, w_o1, b_o1, w_o2, b_o2, direction, w2, b_f2,
+        count, pairs, partial, other, own, w_o1, b_o1, w_o2, b_o2, direction, w2_16, b_f2,
         proj, geom, tangents,
     )
 

time: 74.3 us -> 69.4 us (0.934)
  starting transfers between devices: 32.7 us -> 28.6 us
  Pallas kernels: 20 us -> 18.5 us
  waiting for transfers between devices: 18.6 us -> 20 us
  local copies, waits for them, and re-layouts: 1.92 us -> 0.59 us
    ppermute x11, starting transfers between devices: 32.7 us -> 28.6 us  [exchange(): return lax.ppermute(value, axis, [(i, i ^ step) for i in range(size)])]
    pallas_call x4 -> x7, Pallas kernels: 20 us -> 18.5 us  [run(): pl.pallas_call(kernel, in_specs=specs, out_specs=[pl.BlockSpec(memory_spa...]
    ppermute x11, waiting for transfers between devices: 18.6 us -> 20 us  [exchange(): return lax.ppermute(value, axis, [(i, i ^ step) for i in range(size)])]
    unnamed x6 -> x1, local copies, waits for them, and re-layouts: 1.32 us -> 0.01 us
  transfers between devices with their start and end apart: 11 -> 11, of which waited for: 8 -> 9; matrix products, arithmetic and copies ran while one was open for 1% -> 0% of each run, Pallas kernels for 2% -> 2%
where the time goes in v4:
time: 69.4 us; the launch traced here: 69.1 us
  starting transfers between devices  28.6 us (41%)
  waiting for transfers between devices  20 us (29%)
  Pallas kernels  18.5 us (27%)
  between operations  1.35 us (2%)
    ppermute x11, starting transfers between devices, exchange(): return lax.ppermute(value, axis, [(i, i ^ step) for i in range(size)])  28.6 us
    ppermute x11, waiting for transfers between devices, exchange(): return lax.ppermute(value, axis, [(i, i ^ step) for i in range(size)])  20 us
    pallas_call x7, Pallas kernels, run(): pl.pallas_call(kernel, in_specs=specs, out_specs=[pl.BlockSpec(memory_spa...  18.5 us
  transfers between devices with their start and end apart: 11, of which 9 were waited for; matrix products, arithmetic and copies ran while one was open for 0% of the time, Pallas kernels for 2%

profile of v4, /device:TPU:0, one launch (start us, length us, event | category | flops | bytes accessed | tf_op | source)
XLA Modules:
  0.0 69.1 jit_solution(17345175329557641415)
XLA Ops:
  0.6 0.8 %pack_tile.1 = (bf16[1,144,128]{2,1,0:T(8,128)(2,1)S(1)}, f32[1,8,128]{2,1,0:T(8,128)S(1)}) custom-call(bf16[128,128]{1,0:T(8,128)(2,1)} %features_hbm.1, f32[3,128]{1,0:T(4,128)} %positions_hbm.1), custom_call_target="tpu_custom_call" | custom-call | tf_op jit(solution)/shard_map/pack_tile/pallas_call | solution.py:321
  1.4 3.0 %collective-permute-start.2 = (f32[1,8,128]{2,1,0:T(8,128)S(1)}, f32[1,8,128]{2,1,0:T(8,128)S(1)}, u32[]{:S(2)}, u32[]{:S(2)}) collective-permute-start(f32[1,8,128]{2,1,0:T(8,128)S(1)} %get-tuple-element.29), channel_id=1, source_target_pairs={{0,1},{1,0},{2,3},{3,2},{4,5},{5,4},{6,7},{7,6},{8,9},{9,8},{10,11... | collective-permute-start | bytes 12296 | tf_op jit(solution)/shard_map/ppermute | solution.py:311
  4.4 2.6 %collective-permute-start = (bf16[1,144,128]{2,1,0:T(8,128)(2,1)S(1)}, bf16[1,144,128]{2,1,0:T(8,128)(2,1)S(1)}, u32[]{:S(2)}, u32[]{:S(2)}) collective-permute-start(bf16[1,144,128]{2,1,0:T(8,128)(2,1)S(1)} %get-tuple-element.27.held.near), channel_id=1, source_target_pairs={{0,16},{2,18},{4,20},{6,22},{8,24},{10,26},{12,28},{14,30},{16,0},... | collective-permute-start | bytes 110600 | tf_op jit(solution)/shard_map/ppermute | solution.py:311
  7.0 1.4 %weight_tables.1 = (bf16[256,144]{1,0:T(8,128)(2,1)S(1)}, f32[128,256]{1,0:T(8,128)S(1)}, bf16[128,256]{1,0:T(8,128)(2,1)S(1)}, bf16[128,128]{1,0:T(8,128)(2,1)S...) custom-call(bf16[128,128]{1,0:T(8,128)(2,1)} %w_in_hbm.1, ...), custom_call_target="tpu_custom_call" | custom-call | tf_op jit(solution)/shard_map/weight_tables/pallas_call | solution.py:321
  8.4 0.9 %collective-permute-done.got = bf16[1,144,128]{2,1,0:T(8,128)(2,1)S(1)} collective-permute-done((bf16[1,144,128]{2,1,0:T(8,128)(2,1)S(1)}, bf16[1,144,128]{2,1,0:T(8,128)(2,1)S(1)}, u32[]{:S(2)}, u32[]{:S(2)}) %collective-permute-start) | collective-permute-done | bytes 36896 | tf_op jit(solution)/shard_map/ppermute | solution.py:311
  9.3 1.6 %collective-permute-start.1 = (bf16[2,144,128]{2,1,0:T(8,128)(2,1)S(1)}, bf16[2,144,128]{2,1,0:T(8,128)(2,1)S(1)}, u32[]{:S(2)}, u32[]{:S(2)}) collective-permute-start(bf16[2,144,128]{2,1,0:T(8,128)(2,1)S(1)} %stack_tiles.3.held), channel_id=1, source_target_pairs={{0,8},{2,10},{4,12},{6,14},{8,0},{10,2},{12,4},{14,6},{16,24},{18,... | collective-permute-start | bytes 221192 | tf_op jit(solution)/shard_map/ppermute | solution.py:311
  10.9 0.0 collective-permute-done.2
  10.9 2.8 %collective-permute-done.1.got = bf16[2,144,128]{2,1,0:T(8,128)(2,1)S(1)} collective-permute-done((bf16[2,144,128]{2,1,0:T(8,128)(2,1)S(1)}, bf16[2,144,128]{2,1,0:T(8,128)(2,1)S(1)}, u32[]{:S(2)}, u32[]{:S(2)}) %collective-permute-start.1) | collective-permute-done | bytes 73760 | tf_op jit(solution)/shard_map/ppermute | solution.py:311
  13.7 1.6 %collective-permute-start.3 = (bf16[4,144,128]{2,1,0:T(8,128)(2,1)S(1)}, bf16[4,144,128]{2,1,0:T(8,128)(2,1)S(1)}, u32[]{:S(2)}, u32[]{:S(2)}) collective-permute-start(bf16[4,144,128]{2,1,0:T(8,128)(2,1)S(1)} %stack_tiles.4.held), channel_id=1, source_target_pairs={{0,4},{2,6},{4,0},{6,2},{8,12},{10,14},{12,8},{14,10},{16,20},{18,... | collective-permute-start | bytes 442376 | tf_op jit(solution)/shard_map/ppermute | solution.py:311
  15.2 3.6 %collective-permute-done.3.got = bf16[4,144,128]{2,1,0:T(8,128)(2,1)S(1)} collective-permute-done((bf16[4,144,128]{2,1,0:T(8,128)(2,1)S(1)}, bf16[4,144,128]{2,1,0:T(8,128)(2,1)S(1)}, u32[]{:S(2)}, u32[]{:S(2)}) %collective-permute-start.3) | collective-permute-done | bytes 147488 | tf_op jit(solution)/shard_map/ppermute | solution.py:311
  18.9 0.1 collective-permute-start.4
  19.6 0.9 %collective-permute-done.4.far = bf16[8,144,128]{2,1,0:T(8,128)(2,1)S(1)} collective-permute-done((bf16[8,144,128]{2,1,0:T(8,128)(2,1)S(1)}, bf16[8,144,128]{2,1,0:T(8,128)(2,1)S(1)}, u32[]{:S(2)}, u32[]{:S(2)}) %collective-permute-start.4) | collective-permute-done | bytes 294944 | tf_op jit(solution)/shard_map/ppermute | solution.py:311
  20.5 11.5 %pair_messages.1 = (f32[256,128]{1,0:T(8,128)S(1)}, bf16[256,128]{1,0:T(8,128)(2,1)S(1)}, bf16[4,64,128,256]{3,2,1,0:T(8,128)(2,1)S(1)}, bf16[4,128,128]{2,1,0:T(8,128)(2,1)S(1)}, f32[4,5,64,256]{3,2,1,0:T(8,128)S(1)}) custom-call(s32[1,1]{1,0:T(1,128)S(6)} %copy.18.count, s32[1,1,2,4]{3,2,1,0:T(2,128)S(4)} %get-tuple-element.26.pairs, ...), custom_call_target="tpu_custom_call" | custom-call | tf_op jit(solution)/shard_map/pair_messages/pallas_call | solution.py:321
  32.0 0.6 collective-permute-start.5
  32.6 3.7 %collective-permute-done.5.msg_b = bf16[256,128]{1,0:T(8,128)(2,1)S(1)} collective-permute-done((bf16[256,128]{1,0:T(8,128)(2,1)S(1)}, bf16[256,128]{1,0:T(8,128)(2,1)S(1)}, u32[]{:S(2)}, u32[]{:S(2)}) %collective-permute-start.5) | collective-permute-done | bytes 65568 | tf_op jit(solution)/shard_map/ppermute | solution.py:311
  36.4 4.8 %pair_forces.1 = (bf16[128,128]{1,0:T(8,128)(2,1)}, f32[8,8,128]{2,1,0:T(8,128)S(1)}, f32[8,8,128]{2,1,0:T(8,128)S(1)}, f32[1,8,128]{2,1,0:T(8,128)S(1)}, f32[1,8,128]{2,1,0:T(8,128)S(1)}) custom-call(s32[1,1]{1,0:T(1,128)S(6)} %copy.18.count, s32[1,1,2,4]{3,2,1,0:T(2,128)S(4)} %get-tuple-element.26.pairs, f32[256,128]{1,0:T(8,128)S(1)} %get-tuple-element.34.msg_a, ...), custom_call_target="tpu_custom_call" | custom-call | tf_op jit(solution)/shard_map/pair_forces/pallas_call | solution.py:321
  41.2 0.1 collective-permute-start.6
  41.3 1.2 %collective-permute-done.6 = f32[8,8,128]{2,1,0:T(8,128)S(1)} collective-permute-done((f32[8,8,128]{2,1,0:T(8,128)S(1)}, f32[8,8,128]{2,1,0:T(8,128)S(1)}, u32[]{:S(2)}, u32[]{:S(2)}) %collective-permute-start.6) | collective-permute-done | bytes 32800 | tf_op jit(solution)/shard_map/ppermute | solution.py:311
  42.5 0.0 collective-permute-start.7
  42.5 3.7 %collective-permute-done.7 = f32[4,8,128]{2,1,0:T(8,128)S(1)} collective-permute-done((f32[4,8,128]{2,1,0:T(8,128)S(1)}, f32[4,8,128]{2,1,0:T(8,128)S(1)}, u32[]{:S(2)}, u32[]{:S(2)}) %collective-permute-start.7) | collective-permute-done | bytes 16416 | tf_op jit(solution)/shard_map/ppermute | solution.py:311
  46.2 16.1 %collective-permute-start.8 = (f32[2,8,128]{2,1,0:T(8,128)S(1)}, f32[2,8,128]{2,1,0:T(8,128)S(1)}, u32[]{:S(2)}, u32[]{:S(2)}) collective-permute-start(f32[2,8,128]{2,1,0:T(8,128)S(1)} %get-tuple-element.53), channel_id=1, source_target_pairs={{0,8},{2,10},{4,12},{6,14},{8,0},{10,2},{12,4},{14,6},{16,24},{18,... | collective-permute-start | bytes 24584 | tf_op jit(solution)/shard_map/ppermute | solution.py:311
  62.3 0.0 collective-permute-start.10
  62.3 1.6 %collective-permute-done.8 = f32[2,8,128]{2,1,0:T(8,128)S(1)} collective-permute-done((f32[2,8,128]{2,1,0:T(8,128)S(1)}, f32[2,8,128]{2,1,0:T(8,128)S(1)}, u32[]{:S(2)}, u32[]{:S(2)}) %collective-permute-start.8) | collective-permute-done | bytes 8224 | tf_op jit(solution)/shard_map/ppermute | solution.py:311
  63.9 3.1 %collective-permute-start.9 = (f32[1,8,128]{2,1,0:T(8,128)S(1)}, f32[1,8,128]{2,1,0:T(8,128)S(1)}, u32[]{:S(2)}, u32[]{:S(2)}) collective-permute-start(f32[1,8,128]{2,1,0:T(8,128)S(1)} %slice_add_fusion.4), channel_id=1, source_target_pairs={{0,16},{2,18},{4,20},{6,22},{8,24},{10,26},{12,28},{14,30},{16,0},... | collective-permute-start | bytes 12296 | tf_op jit(solution)/shard_map/ppermute | solution.py:311
  67.0 0.0 collective-permute-done.10
  67.0 1.6 %collective-permute-done.9 = f32[1,8,128]{2,1,0:T(8,128)S(1)} collective-permute-done((f32[1,8,128]{2,1,0:T(8,128)S(1)}, f32[1,8,128]{2,1,0:T(8,128)S(1)}, u32[]{:S(2)}, u32[]{:S(2)}) %collective-permute-start.9) | collective-permute-done | bytes 4128 | tf_op jit(solution)/shard_map/ppermute | solution.py:311
  68.6 0.6 slice_bitcast_fusion
  (9 shorter events, 0.1 us)
Async XLA Ops:
  1.4 9.4 %collective-permute-start.2 = (f32[1,8,128]{2,1,0:T(8,128)S(1)}, f32[1,8,128]{2,1,0:T(8,128)S(1)}, u32[]{:S(2)}, u32[]{:S(2)}) collective-permute-start(f32[1,8,128]{2,1,0:T(8,128)S(1)} %get-tuple-element.29), channel_id=1, source_target_pairs={{0,1},{1,0},{2,3},{3,2},{4,5},{5,4},{6,7},{7,6},{8,9},{9,8},{10,11... | collective-permute-start | bytes 12296 | tf_op jit(solution)/shard_map/ppermute | solution.py:311
  4.4 4.9 %collective-permute-start = (bf16[1,144,128]{2,1,0:T(8,128)(2,1)S(1)}, bf16[1,144,128]{2,1,0:T(8,128)(2,1)S(1)}, u32[]{:S(2)}, u32[]{:S(2)}) collective-permute-start(bf16[1,144,128]{2,1,0:T(8,128)(2,1)S(1)} %get-tuple-element.27.held.near), channel_id=1, source_target_pairs={{0,16},{2,18},{4,20},{6,22},{8,24},{10,26},{12,28},{14,30},{16,0},... | collective-permute-start | bytes 110600 | tf_op jit(solution)/shard_map/ppermute | solution.py:311
  9.3 4.4 %collective-permute-start.1 = (bf16[2,144,128]{2,1,0:T(8,128)(2,1)S(1)}, bf16[2,144,128]{2,1,0:T(8,128)(2,1)S(1)}, u32[]{:S(2)}, u32[]{:S(2)}) collective-permute-start(bf16[2,144,128]{2,1,0:T(8,128)(2,1)S(1)} %stack_tiles.3.held), channel_id=1, source_target_pairs={{0,8},{2,10},{4,12},{6,14},{8,0},{10,2},{12,4},{14,6},{16,24},{18,... | collective-permute-start | bytes 221192 | tf_op jit(solution)/shard_map/ppermute | solution.py:311
  13.7 5.2 %collective-permute-start.3 = (bf16[4,144,128]{2,1,0:T(8,128)(2,1)S(1)}, bf16[4,144,128]{2,1,0:T(8,128)(2,1)S(1)}, u32[]{:S(2)}, u32[]{:S(2)}) collective-permute-start(bf16[4,144,128]{2,1,0:T(8,128)(2,1)S(1)} %stack_tiles.4.held), channel_id=1, source_target_pairs={{0,4},{2,6},{4,0},{6,2},{8,12},{10,14},{12,8},{14,10},{16,20},{18,... | collective-permute-start | bytes 442376 | tf_op jit(solution)/shard_map/ppermute | solution.py:311
  18.9 1.6 %collective-permute-start.4 = (bf16[8,144,128]{2,1,0:T(8,128)(2,1)S(1)}, bf16[8,144,128]{2,1,0:T(8,128)(2,1)S(1)}, u32[]{:S(2)}, u32[]{:S(2)}) collective-permute-start(bf16[8,144,128]{2,1,0:T(8,128)(2,1)S(1)} %stack_tiles.5.near), channel_id=1, source_target_pairs={{0,2},{2,0},{4,6},{6,4},{8,10},{10,8},{12,14},{14,12},{16,18},{18,... | collective-permute-start | bytes 884744 | tf_op jit(solution)/shard_map/ppermute | solution.py:311
  32.0 4.3 %collective-permute-start.5 = (bf16[256,128]{1,0:T(8,128)(2,1)S(1)}, bf16[256,128]{1,0:T(8,128)(2,1)S(1)}, u32[]{:S(2)}, u32[]{:S(2)}) collective-permute-start(bf16[256,128]{1,0:T(8,128)(2,1)S(1)} %get-tuple-element.35), channel_id=1, source_target_pairs={{0,1},{1,0},{2,3},{3,2},{4,5},{5,4},{6,7},{7,6},{8,9},{9,8},{10,11... | collective-permute-start | bytes 196616 | tf_op jit(solution)/shard_map/ppermute | solution.py:311
  41.2 1.3 %collective-permute-start.6 = (f32[8,8,128]{2,1,0:T(8,128)S(1)}, f32[8,8,128]{2,1,0:T(8,128)S(1)}, u32[]{:S(2)}, u32[]{:S(2)}) collective-permute-start(f32[8,8,128]{2,1,0:T(8,128)S(1)} %get-tuple-element.47), channel_id=1, source_target_pairs={{0,2},{2,0},{4,6},{6,4},{8,10},{10,8},{12,14},{14,12},{16,18},{18,... | collective-permute-start | bytes 98312 | tf_op jit(solution)/shard_map/ppermute | solution.py:311
  42.5 3.7 %collective-permute-start.7 = (f32[4,8,128]{2,1,0:T(8,128)S(1)}, f32[4,8,128]{2,1,0:T(8,128)S(1)}, u32[]{:S(2)}, u32[]{:S(2)}) collective-permute-start(f32[4,8,128]{2,1,0:T(8,128)S(1)} %get-tuple-element.51), channel_id=1, source_target_pairs={{0,4},{2,6},{4,0},{6,2},{8,12},{10,14},{12,8},{14,10},{16,20},{18,... | collective-permute-start | bytes 49160 | tf_op jit(solution)/shard_map/ppermute | solution.py:311
  46.2 17.7 %collective-permute-start.8 = (f32[2,8,128]{2,1,0:T(8,128)S(1)}, f32[2,8,128]{2,1,0:T(8,128)S(1)}, u32[]{:S(2)}, u32[]{:S(2)}) collective-permute-start(f32[2,8,128]{2,1,0:T(8,128)S(1)} %get-tuple-element.53), channel_id=1, source_target_pairs={{0,8},{2,10},{4,12},{6,14},{8,0},{10,2},{12,4},{14,6},{16,24},{18,... | collective-permute-start | bytes 24584 | tf_op jit(solution)/shard_map/ppermute | solution.py:311
  62.3 4.7 %collective-permute-start.10 = (f32[1,8,128]{2,1,0:T(8,128)S(1)}, f32[1,8,128]{2,1,0:T(8,128)S(1)}, u32[]{:S(2)}, u32[]{:S(2)}) collective-permute-start(f32[1,8,128]{2,1,0:T(8,128)S(1)} %get-tuple-element.49), channel_id=1, source_target_pairs={{0,1},{1,0},{2,3},{3,2},{4,5},{5,4},{6,7},{7,6},{8,9},{9,8},{10,11... | collective-permute-start | bytes 12296 | tf_op jit(solution)/shard_map/ppermute | solution.py:311
  63.9 4.6 %collective-permute-start.9 = (f32[1,8,128]{2,1,0:T(8,128)S(1)}, f32[1,8,128]{2,1,0:T(8,128)S(1)}, u32[]{:S(2)}, u32[]{:S(2)}) collective-permute-start(f32[1,8,128]{2,1,0:T(8,128)S(1)} %slice_add_fusion.4), channel_id=1, source_target_pairs={{0,16},{2,18},{4,20},{6,22},{8,24},{10,26},{12,28},{14,30},{16,0},... | collective-permute-start | bytes 12296 | tf_op jit(solution)/shard_map/ppermute | solution.py:311
